TPU v7x, 768 devices: a whole 4x8x12 slice. The times are simulated.
768 devices in a mesh: em: 12 (over z), blk: 4 (over x), rep: 16 (over y, core).
Axes of the slice: x: 4, y: 8, z: 12, core: 2. Of those that a mesh axis runs over, the one named last changes fastest.
Arguments:
- green: bfloat16 [768, 4, 8, 128, 256], P(('em', 'rep'), None, 'blk'), may hold values from -6 to 6
- occupation: float32 [4], replicated, may hold values from 0.2 to 4
- offsets: int32 [4], replicated, may hold values from 1 to 2, as said below
- qtable: int32 [4, 4], replicated, may hold values from 0 to 3
- coupling: bfloat16 [8, 3, 128, 128], P('blk'), may hold values from -0.5 to 0.5
- pattern: int32 [8, 3], P('blk'), may hold values 0 or 1
Outputs:
- sigma: bfloat16 [768, 4, 8, 128, 256], P(('em', 'rep'), None, 'blk')
Inputs may be any that keep to these rules, and one draw needn't show every extreme that they name: `offsets`: every offset lies in 1 .. 2 and one equals 2.
All inputs are finite; a program needn't handle non-finite values. No bound on the sum of `pattern` on one device may be relied on, other than what follows from the above.
Results may differ from a plain program's by a relative error of at most 0.0057.
Values may be sent and summed in bfloat16 or wider, within the bound.
No kernel may reach another device: no remote copies, remote signals or barrier semaphores. Data moves between devices by JAX's collectives and lax.ppermute only.
A program may use at most 64 MiB of HBM per device.

v0:
```python
import jax
import jax.numpy as jnp
from jax import lax
from jax.sharding import PartitionSpec as P

OFF_MAX = 2


def extended_2(block, sides, width):
    for axis, dim in sides:
        count = lax.axis_size(axis)
        forward = [(i, i + 1) for i in range(count - 1)]
        backward = [(target, source) for source, target in forward]
        low = lax.ppermute(
            lax.slice_in_dim(block, block.shape[dim] - width, None, axis=dim), axis, forward
        )
        high = lax.ppermute(lax.slice_in_dim(block, 0, width, axis=dim), axis, backward)
        block = jnp.concatenate([low, block, high], axis=dim)
    return block


def aggregate(weights, source, e_count, k_count):
    tiles = source.shape[2]
    rows = source.shape[3]
    columns = source.shape[4]
    flat = source.reshape(source.shape[0] * k_count, -1)
    result = jnp.dot(weights, flat, preferred_element_type=jnp.float32).astype(jnp.bfloat16)
    return result.reshape(e_count, k_count, tiles, rows, columns)


def local(green, occupation, offsets, qtable, coupling, pattern):
    e_count, k_count, t_count, orbitals, columns = green.shape
    reach = OFF_MAX
    extended = extended_2(green, ((("em", "rep"), 0),), reach)
    shifts = jnp.arange(2 * reach + 1, dtype=jnp.int32) - reach
    hits_up = (offsets[:, None] == shifts[None, :]).astype(jnp.float32)
    hits_down = (offsets[:, None] == -shifts[None, :]).astype(jnp.float32)
    band = jnp.sum((occupation[:, None] + 1.0) * hits_up + occupation[:, None] * hits_down, axis=0)
    momenta = jnp.arange(k_count, dtype=jnp.int32)
    transfer = (
        jnp.sum((qtable[:, :, None] == momenta[None, None, :]).astype(jnp.float32), axis=1)
        / qtable.shape[1]
    )
    kern = (band[:, None, None] * transfer[None, :, :]).astype(jnp.bfloat16)
    spacing = jnp.arange(e_count + 2 * reach)[None, :] - jnp.arange(e_count)[:, None] - reach
    select = (spacing[None, :, :] == shifts[:, None, None]).astype(jnp.bfloat16)
    weights = jnp.einsum("dab,dkl->akbl", select, kern, preferred_element_type=jnp.float32).astype(
        jnp.bfloat16
    )
    weights = weights.reshape(e_count * k_count, (e_count + 2 * reach) * k_count)
    agg = aggregate(weights, extended, e_count, k_count)
    rimmed = extended_2(agg, (("blk", 2),), 1)
    masked = coupling * pattern[:, :, None, None].astype(jnp.bfloat16)
    whole = masked.astype(jnp.float32)
    sigma = jnp.zeros((e_count, k_count, t_count, orbitals, 2, orbitals), jnp.float32)
    for near in range(3):
        nearby = rimmed[:, :, near : near + t_count]
        left = jnp.einsum(
            "tdr,ektrc->ektdc", masked[:, near], nearby, preferred_element_type=jnp.float32
        )
        left = left.reshape(e_count, k_count, t_count, orbitals, 2, orbitals)
        sigma = sigma + jnp.einsum(
            "ektdpc,tfc->ektdpf", left, whole[:, near], precision=lax.Precision.HIGHEST
        )
    return sigma.reshape(e_count, k_count, t_count, orbitals, columns).astype(jnp.bfloat16)


def solution(mesh):
    in_specs = (
        P(("em", "rep"), None, "blk", None, None),
        P(),
        P(),
        P(),
        P("blk", None, None, None),
        P("blk", None),
    )
    out_specs = P(("em", "rep"), None, "blk", None, None)
    return jax.shard_map(local, mesh=mesh, in_specs=in_specs, out_specs=out_specs, check_vma=False)
```

profile of v0, /device:TPU:509, one launch (start us, length us, event | category | flops | bytes accessed | tf_op | source)
XLA Modules:
  0.0 76.5 jit_solution(11278300032977733330)
XLA Ops:
  0.0 0.0 copy-start.4
  0.0 0.0 copy-start.5
  0.0 2.8 %fusion.36 = (bf16[2,4,2,128,256]{4,3,2,1,0:T(8,128)(2,1)S(1)}, bf16[2,4,2,128,256]{4,3,2,1,0:T(8,128)(2,1)}) fusion(bf16[4,4,2,128,256]{4,3,2,1,0:T(8,128)(2,1)} %param.6), kind=kLoop, calls=%fused_computation.48 | loop fusion | bytes 4194304 | tf_op jit(solution)/shard_map/slice | solution.py:15
  2.9 2.6 %collective-permute-start.1 = (bf16[2,4,2,128,256]{4,3,2,1,0:T(8,128)(2,1)}, bf16[2,4,2,128,256]{4,3,2,1,0:T(8,128)(2,1)}, u32[]{:S(2)}, u32[]{:S(2)}) collective-permute-start(bf16[2,4,2,128,256]{4,3,2,1,0:T(8,128)(2,1)} %get-tuple-element.8), channel_id=1, source_target_pairs={{1,0},{2,1},{3,2},{4,3},{5,4},{6,5},{7,6},{8,7},{9,8},{10,9},{11,1... | collective-permute-start | bytes 3145736 | tf_op jit(solution)/shard_map/ppermute | solution.py:17
  5.4 6.3 %collective-permute-start = (bf16[2,4,2,128,256]{4,3,2,1,0:T(8,128)(2,1)S(1)}, bf16[2,4,2,128,256]{4,3,2,1,0:T(8,128)(2,1)}, u32[]{:S(2)}, u32[]{:S(2)}) collective-permute-start(bf16[2,4,2,128,256]{4,3,2,1,0:T(8,128)(2,1)S(1)} %get-tuple-element.7), channel_id=1, source_target_pairs={{0,1},{1,2},{2,3},{3,4},{4,5},{5,6},{6,7},{7,8},{8,9},{9,10},{10,1... | collective-permute-start | bytes 3145736 | tf_op jit(solution)/shard_map/ppermute | solution.py:14
  11.8 0.1 convert_reduce_fusion
  11.9 0.0 copy-done.4
  11.9 0.1 add_reduce_fusion
  12.0 0.2 fusion.8
  12.2 0.2 copy.32
  12.4 0.1 reshape.56
  12.5 0.1 copy.30
  12.6 10.0 %collective-permute-done.1 = bf16[2,4,2,128,256]{4,3,2,1,0:T(8,128)(2,1)} collective-permute-done((bf16[2,4,2,128,256]{4,3,2,1,0:T(8,128)(2,1)}, bf16[2,4,2,128,256]{4,3,2,1,0:T(8,128)(2,1)}, u32[]{:S(2)}, u32[]{:S(2)}) %collective-permute-start.1) | collective-permute-done | bytes 1048608 | tf_op jit(solution)/shard_map/ppermute | solution.py:17
  22.6 0.9 %collective-permute-done = bf16[2,4,2,128,256]{4,3,2,1,0:T(8,128)(2,1)} collective-permute-done((bf16[2,4,2,128,256]{4,3,2,1,0:T(8,128)(2,1)S(1)}, bf16[2,4,2,128,256]{4,3,2,1,0:T(8,128)(2,1)}, u32[]{:S(2)}, u32[]{:S(2)}) %collective-permute-start) | collective-permute-done | bytes 1048608 | tf_op jit(solution)/shard_map/ppermute | solution.py:14
  23.5 3.4 %pad_maximum_fusion = bf16[8,4,2,128,256]{4,3,2,1,0:T(8,128)(2,1)} fusion(bf16[2,4,2,128,256]{4,3,2,1,0:T(8,128)(2,1)} %collective-permute-done.1, bf16[4,4,2,128,256]{4,3,2,1,0:T(8,128)(2,1)S(1)} %copy-done, bf16[2,4,2,128,256]{4,3,2,1,0:T(8,128)(2,1)} %collective-permute-done), kind=kLoop, calls=%fused_computation.1 | loop fusion | flops 4194304 | bytes 8388608 | tf_op jit(solution)/shard_map/concatenate | solution.py:18
  26.9 5.7 %reshape.57 = bf16[32,65536]{1,0:T(8,128)(2,1)} reshape(bf16[8,4,2,128,256]{4,3,2,1,0:T(8,128)(2,1)} %pad_maximum_fusion) | data formatting | bytes 8388608 | tf_op jit(solution)/shard_map/reshape | solution.py:26
  32.5 2.9 %convolution_convert_fusion = bf16[16,65536]{1,0:T(8,128)(2,1)S(1)} fusion(bf16[16,32]{1,0:T(8,128)(2,1)S(1)} %reshape.56, bf16[32,65536]{1,0:T(8,128)(2,1)} %reshape.57), kind=kOutput, calls=%fused_computation | convolution fusion | flops 68157440 | bytes 6292480 | tf_op jit(solution)/shard_map/dot_general | solution.py:27
  35.4 1.8 %copy.54 = bf16[2,8,256,256]{3,2,1,0:T(8,128)(2,1)} copy(bf16[2,8,256,256]{3,1,2,0:T(8,128)(2,1)S(1)} %bitcast.79) | data formatting | bytes 4194304
  37.2 3.0 %copy.33 = bf16[4,4,2,128,256]{3,4,1,0,2:T(8,128)(2,1)S(1)} copy(bf16[4,4,2,128,256]{4,3,2,1,0:T(8,128)(2,1)} %bitcast.78) | data formatting | bytes 4194304 | tf_op jit(solution)/shard_map/reshape | solution.py:28
  40.2 0.2 fusion.35
  40.5 2.8 %collective-permute-start.2 = (bf16[4,4,1,128,256]{3,4,1,0,2:T(8,128)(2,1)S(1)}, bf16[4,4,1,128,256]{3,4,1,0,2:T(8,128)(2,1)S(1)}, u32[]{:S(2)}, u32[]{:S(2)}) collective-permute-start(bf16[4,4,1,128,256]{3,4,1,0,2:T(8,128)(2,1)S(1)} %get-tuple-element.6), channel_id=1, source_target_pairs={{0,16},{16,32},{32,48},{1,17},{17,33},{33,49},{2,18},{18,34},{34,5... | collective-permute-start | bytes 3145736 | tf_op jit(solution)/shard_map/ppermute | solution.py:14
  43.3 0.1 copy_multiply_fusion
  43.4 2.6 %collective-permute-start.3 = (bf16[4,4,1,128,256]{3,4,1,0,2:T(8,128)(2,1)S(1)}, bf16[4,4,1,128,256]{3,4,1,0,2:T(8,128)(2,1)S(1)}, u32[]{:S(2)}, u32[]{:S(2)}) collective-permute-start(bf16[4,4,1,128,256]{3,4,1,0,2:T(8,128)(2,1)S(1)} %get-tuple-element.5), channel_id=1, source_target_pairs={{16,0},{32,16},{48,32},{17,1},{33,17},{49,33},{18,2},{34,18},{50,3... | collective-permute-start | bytes 3145736 | tf_op jit(solution)/shard_map/ppermute | solution.py:17
  46.0 0.7 fusion.11
  46.7 2.4 %fusion.13 = f32[2,128,4,4,128,2]{4,1,5,3,2,0:T(8,128)S(1)} fusion(f32[4,4,2,128,2,128]{3,5,4,1,0,2:T(8,128)S(1)} %bitcast.76, bf16[2,3,128,128]{3,2,0,1:T(8,128)(2,1)S(1)} %copy_multiply_fusion), kind=kOutput, calls=%fused_computation.18 | convolution fusion | flops 1610612736 | bytes 8454144 | tf_op jit(solution)/shard_map/ektdpc,tfc->ektdpf/dot_general | solution.py:62
  49.2 17.8 %collective-permute-done.2 = bf16[4,4,1,128,256]{3,4,1,0,2:T(8,128)(2,1)S(1)} collective-permute-done((bf16[4,4,1,128,256]{3,4,1,0,2:T(8,128)(2,1)S(1)}, bf16[4,4,1,128,256]{3,4,1,0,2:T(8,128)(2,1)S(1)}, u32[]{:S(2)}, u32[]{:S(2)}) %collective-permute-start.2) | collective-permute-done | bytes 1048608 | tf_op jit(solution)/shard_map/ppermute | solution.py:14
  67.0 0.7 fusion
  67.7 2.4 %fusion.16 = f32[2,128,4,4,128,2]{4,1,5,3,2,0:T(8,128)S(1)} fusion(f32[4,4,2,128,2,128]{3,5,4,1,0,2:T(8,128)S(1)} %bitcast.75, bf16[2,3,128,128]{3,2,0,1:T(8,128)(2,1)S(1)} %copy_multiply_fusion), kind=kOutput, calls=%fused_computation.21 | convolution fusion | flops 1610612736 | bytes 8454144 | tf_op jit(solution)/shard_map/ektdpc,tfc->ektdpf/dot_general | solution.py:62
  70.1 0.0 collective-permute-done.3
  70.1 0.8 %fusion.4 = f32[2,4,4,256,128]{4,3,2,1,0:T(8,128)S(1)} fusion(bf16[4,4,1,128,256]{3,4,1,0,2:T(8,128)(2,1)S(1)} %collective-permute-done.3, bf16[4,4,2,128,256]{3,4,1,0,2:T(8,128)(2,1)S(1)} %copy.33, bf16[2,3,128,128]{3,2,0,1:T(8,128)(2,1)S(1)} %copy_multiply_fusion), kind=kOutput, calls=%fused_computation.7 | convolution fusion | flops 274726912 | bytes 7405568 | tf_op jit(solution)/shard_map/tdr,ektrc->ektdc/dot_general | solution.py:58
  70.9 3.2 %add_convert_fusion = bf16[2,128,4,4,128,2]{4,1,5,3,2,0:T(8,128)(2,1)S(1)} fusion(f32[2,128,4,4,128,2]{4,1,5,3,2,0:T(8,128)S(1)} %fusion.16, f32[2,128,4,4,128,2]{4,1,5,3,2,0:T(8,128)S(1)} %fusion.13, f32[4,4,2,128,2,128]{3,5,4,1,0,2:T(8,128)S(1)} %bitcast.74, bf16[2,3,128,128]{3,2,0,1:T(8,128)(2,1)S(1)} %copy_multiply_fusion), kind=kOutput, calls=%fused_computation.2 | convolution fusion | flops 1613758464 | bytes 14745600 | tf_op jit(solution)/shard_map/ektdpc,tfc->ektdpf/dot_general | solution.py:62
  74.2 2.3 %copy.41 = bf16[4,4,2,128,256]{4,3,2,1,0:T(8,128)(2,1)} copy(bf16[4,4,2,128,256]{3,4,1,0,2:T(8,128)(2,1)S(1)} %bitcast.77) | data formatting | bytes 4194304 | tf_op jit(solution)/shard_map/convert_element_type | solution.py:65
  (14 shorter events, 0.0 us)
Async XLA Ops:
  0.0 23.5 %copy-start = (bf16[4,4,2,128,256]{4,3,2,1,0:T(8,128)(2,1)S(1)}, bf16[4,4,2,128,256]{4,3,2,1,0:T(8,128)(2,1)}, u32[]{:S(2)}) copy-start(bf16[4,4,2,128,256]{4,3,2,1,0:T(8,128)(2,1)} %param.6) | copy-start | bytes 6291460
  0.0 11.8 %copy-start.2 = (s32[4,4]{1,0:T(4,128)S(1)}, s32[4,4]{1,0:T(4,128)}, u32[]{:S(2)}) copy-start(s32[4,4]{1,0:T(4,128)} %param.9) | copy-start | bytes 196
  0.0 11.9 %copy-start.3 = (f32[4]{0:T(128)S(1)}, f32[4]{0:T(128)}, u32[]{:S(2)}) copy-start(f32[4]{0:T(128)} %param.7) | copy-start | bytes 52
  0.0 11.9 %copy-start.4 = (s32[4]{0:T(128)S(1)}, s32[4]{0:T(128)}, u32[]{:S(2)}) copy-start(s32[4]{0:T(128)} %param.8) | copy-start | bytes 52
  0.0 12.5 %copy-start.5 = (s32[2,3]{1,0:T(2,128)S(1)}, s32[2,3]{1,0:T(2,128)}, u32[]{:S(2)}) copy-start(s32[2,3]{1,0:T(2,128)} %param.11) | copy-start | bytes 76
  2.9 19.7 %collective-permute-start.1 = (bf16[2,4,2,128,256]{4,3,2,1,0:T(8,128)(2,1)}, bf16[2,4,2,128,256]{4,3,2,1,0:T(8,128)(2,1)}, u32[]{:S(2)}, u32[]{:S(2)}) collective-permute-start(bf16[2,4,2,128,256]{4,3,2,1,0:T(8,128)(2,1)} %get-tuple-element.8), channel_id=1, source_target_pairs={{1,0},{2,1},{3,2},{4,3},{5,4},{6,5},{7,6},{8,7},{9,8},{10,9},{11,1... | collective-permute-start | bytes 3145736 | tf_op jit(solution)/shard_map/ppermute | solution.py:17
  5.4 18.0 %collective-permute-start = (bf16[2,4,2,128,256]{4,3,2,1,0:T(8,128)(2,1)S(1)}, bf16[2,4,2,128,256]{4,3,2,1,0:T(8,128)(2,1)}, u32[]{:S(2)}, u32[]{:S(2)}) collective-permute-start(bf16[2,4,2,128,256]{4,3,2,1,0:T(8,128)(2,1)S(1)} %get-tuple-element.7), channel_id=1, source_target_pairs={{0,1},{1,2},{2,3},{3,4},{4,5},{5,6},{6,7},{7,8},{8,9},{9,10},{10,1... | collective-permute-start | bytes 3145736 | tf_op jit(solution)/shard_map/ppermute | solution.py:14
  37.2 6.1 %copy-start.1 = (bf16[2,3,128,128]{3,2,1,0:T(8,128)(2,1)S(1)}, bf16[2,3,128,128]{3,2,1,0:T(8,128)(2,1)}, u32[]{:S(2)}) copy-start(bf16[2,3,128,128]{3,2,1,0:T(8,128)(2,1)} %param.10) | copy-start | bytes 589828
  40.5 26.5 %collective-permute-start.2 = (bf16[4,4,1,128,256]{3,4,1,0,2:T(8,128)(2,1)S(1)}, bf16[4,4,1,128,256]{3,4,1,0,2:T(8,128)(2,1)S(1)}, u32[]{:S(2)}, u32[]{:S(2)}) collective-permute-start(bf16[4,4,1,128,256]{3,4,1,0,2:T(8,128)(2,1)S(1)} %get-tuple-element.6), channel_id=1, source_target_pairs={{0,16},{16,32},{32,48},{1,17},{17,33},{33,49},{2,18},{18,34},{34,5... | collective-permute-start | bytes 3145736 | tf_op jit(solution)/shard_map/ppermute | solution.py:14
  43.4 26.7 %collective-permute-start.3 = (bf16[4,4,1,128,256]{3,4,1,0,2:T(8,128)(2,1)S(1)}, bf16[4,4,1,128,256]{3,4,1,0,2:T(8,128)(2,1)S(1)}, u32[]{:S(2)}, u32[]{:S(2)}) collective-permute-start(bf16[4,4,1,128,256]{3,4,1,0,2:T(8,128)(2,1)S(1)} %get-tuple-element.5), channel_id=1, source_target_pairs={{16,0},{32,16},{48,32},{17,1},{33,17},{49,33},{18,2},{34,18},{50,3... | collective-permute-start | bytes 3145736 | tf_op jit(solution)/shard_map/ppermute | solution.py:17
where the time goes:
time: 77 us; the launch traced here: 76.5 us
  waiting for transfers between devices  28.7 us (37%)
  local copies, waits for them, and re-layouts  16.3 us (21%)
  starting transfers between devices  14.3 us (19%)
  matrix products  13.3 us (17%)
  other arithmetic  3.67 us (5%)
    ppermute x2, waiting for transfers between devices, extended_2(): lax.ppermute(lax.slice_in_dim(block, block.shape[dim] - width, None, axis...  18.7 us
    ppermute x2, waiting for transfers between devices, extended_2(): lax.ppermute(lax.slice_in_dim(block, 0, width, axis=dim), axis, backward)  10 us
    ppermute x2, starting transfers between devices, extended_2(): lax.ppermute(lax.slice_in_dim(block, block.shape[dim] - width, None, axis...  9.14 us
    dot_general x3, matrix products, local(): jnp.einsum('ektdpc,tfc->ektdpf', left, whole[:, near], precision=lax.Prec...  8.03 us
    reshape x1, local copies, waits for them, and re-layouts, aggregate(): flat = source.reshape(source.shape[0] * k_count, -1)  5.65 us
    ppermute x2, starting transfers between devices, extended_2(): lax.ppermute(lax.slice_in_dim(block, 0, width, axis=dim), axis, backward)  5.2 us
    concatenate x1, other arithmetic, extended_2(): block = jnp.concatenate([low, block, high], axis=dim)  3.39 us
    reshape x1, local copies, waits for them, and re-layouts, aggregate(): return result.reshape(e_count, k_count, tiles, rows, columns)  3.03 us
  transfers between devices with their start and end apart: 4, of which 3 were waited for; matrix products, arithmetic and copies ran while one was open for 9% of the time, Pallas kernels for 0%

commit v1 on v0

v1 whole, which is shorter than its diff:
```python
import jax
import jax.numpy as jnp
from jax import lax
from jax.experimental import pallas as pl
from jax.experimental.pallas import tpu as pltpu
from jax.sharding import PartitionSpec as P

REACH = 2
FIRST = 64
VMEM = pl.BlockSpec(memory_space=pltpu.VMEM)
SMEM = pl.BlockSpec(memory_space=pltpu.SMEM)
ANY = pl.BlockSpec(memory_space=pl.ANY)
PARAMS = pltpu.CompilerParams(vmem_limit_bytes=40 * 2**20)
BF16 = jnp.bfloat16


def swap_pairs(count, first):
    pairs = [(i, i + 1) for i in range(first, count - 1, 2)]
    return pairs + [(b, a) for a, b in pairs]


def edge_kernel(s_ref, green, first2, whole1, second2):
    rows = first2.shape[3]
    one, two = 2 - 2 * s_ref[2], 2 * s_ref[2]
    for e in range(REACH):
        first2[e] = green[two + e, :, :, :rows]
        whole1[e] = green[one + e]
        second2[e] = green[two + e, :, :, rows:]


def weight_kernel(s_ref, occupation, offsets, qtable, out):
    def band(d):
        total = 0.0
        for s in range(4):
            value = occupation[s] + 1.0 if d > 0 else occupation[s]
            total = total + jnp.where(offsets[s] == abs(d), value, 0.0)
        return total

    bands = {d: band(d) for d in (-2, -1, 1, 2)}
    lane = lax.broadcasted_iota(jnp.int32, (16, 128), 1)
    unit = lax.broadcasted_iota(jnp.int32, (16, 128), 0) == lane % 16
    transfer = []
    for k in range(4):
        row = jnp.zeros((16, 128), jnp.float32)
        for l in range(4):
            hits = sum(jnp.where(qtable[k, q] == l, 0.25, 0.0) for q in range(4))
            row = jnp.where(unit & ((lane // 16) % 4 == l), hits, row)
        transfer.append(row)

    def weight(even, odd):
        low, high = bands.get(even, 0.0), bands.get(odd, 0.0)
        return jnp.where(s_ref[2] == 1, high, low)

    for place, (even, odd) in enumerate(((4, -2), (0, 0), (2, 2), (-2, 4))):
        for e in range(4):
            left = weight(even - e, odd - e)
            right = weight(even - e + 1, odd - e + 1)
            scale = jnp.where(lane < 64, left, right)
            for k in range(4):
                at = pl.ds(64 * e + 16 * k, 16)
                out[at, place * 128 : (place + 1) * 128] = (scale * transfer[k]).astype(BF16)


def aggregate_rows(weights, side1, own, side2, out, out_row):
    blocks = [side1(e, l) for e in range(2) for l in range(4)]
    blocks += [own(e, l) for e in range(4) for l in range(4)]
    blocks += [side2(e, l) for e in range(2) for l in range(4)]
    total = jnp.dot(
        weights[...], jnp.concatenate(blocks, axis=0), preferred_element_type=jnp.float32
    ).astype(BF16)
    for e in range(4):
        for k in range(4):
            n = 16 * (4 * e + k)
            out[e, k, pl.ds(out_row, 16)] = total[n : n + 16]


def own_kernel(row, s_ref, weights, green, side1, side2, out1, out2):
    for slot, out in ((0, out1), (1, out2)):
        tile = s_ref[slot]

        def step(n, carry):
            r = pl.multiple_of(n * 16, 16)
            aggregate_rows(
                weights,
                lambda e, l: side1[e, l, tile, pl.ds(r + row, 16)],
                lambda e, l: green[e, l, tile, pl.ds(r + row, 16)],
                lambda e, l: side2[e, l, tile, pl.ds(r, 16)],
                out,
                r,
            )
            return carry

        lax.fori_loop(0, out.shape[2] // 16, step, 0, unroll=4)


TRANSPOSED = (((1,), (1,)), ((), ()))


def right_products(part, weight, p):
    rows = part.shape[2]
    lhs = part[:, :, :, p * 128 : (p + 1) * 128].reshape(16 * rows, 128)
    u = lax.dot_general(lhs, weight, TRANSPOSED, preferred_element_type=jnp.float32)
    return u.astype(BF16).reshape(16, rows, weight.shape[0])


def inner_kernel(s_ref, eff, first1, second1, first2, second2, out, work):
    tau = [s_ref[0], s_ref[1]]
    pair = [
        jnp.concatenate([eff[tau[0], 1], eff[tau[1], 2 - 2 * tau[1]]], axis=0),
        jnp.concatenate([eff[tau[0], 2 - 2 * tau[0]], eff[tau[1], 1]], axis=0),
    ]
    raw = first1.shape[2]
    for source, parts in enumerate(((first1, second1), (first2, second2))):
        for part, row in zip(parts, (0, raw)):
            for p in range(2):
                u = right_products(part, pair[source], p)
                at = pl.ds(source * 128 + row, part.shape[2])
                for a in range(2):
                    work[a, :, at, p * 128 : (p + 1) * 128] = u[:, :, a * 128 : (a + 1) * 128]
    stack = [
        jnp.concatenate([eff[tau[0], 1], eff[tau[0], 2 - 2 * tau[0]]], axis=1),
        jnp.concatenate([eff[tau[1], 2 - 2 * tau[1]], eff[tau[1], 1]], axis=1),
    ]

    def step(e, carry):
        for k in range(4):
            for a in range(2):
                out[e, k, a] = jnp.dot(
                    stack[a], work[a, 4 * e + k], preferred_element_type=jnp.float32
                )
        return carry

    lax.fori_loop(0, 4, step, 0, unroll=2)


def half_kernel(s_ref, eff, first1, first2, out):
    for a, part in enumerate((first1, first2)):
        rim = eff[s_ref[a], 2 * s_ref[a]]
        for p in range(2):
            out[a, :, :, p * 128 : (p + 1) * 128] = right_products(part, rim, p)


def final_kernel(s_ref, eff, inner, half, second1, second2, out, work, store, sems):
    tau = [s_ref[0], s_ref[1]]
    rim = [eff[tau[a], 2 * tau[a]] for a in range(2)]
    for a, part in enumerate((second1, second2)):
        for p in range(2):
            work[a, :, :, p * 128 : (p + 1) * 128] = right_products(part, rim[a], p)

    copies = []
    for e in range(4):
        for k in range(4):
            for a in range(2):
                right = jnp.concatenate([half[a, 4 * e + k], work[a, 4 * e + k]], axis=0)
                total = jnp.dot(rim[a], right, preferred_element_type=jnp.float32)
                store[e, k, tau[a]] = (inner[e, k, a] + total).astype(BF16)
        copies.append(pltpu.make_async_copy(store.at[e], out.at[e], sems.at[e]))
        copies[-1].start()
    for copy in copies:
        copy.wait()


def call(kernel, in_specs, shapes, args, name, out_specs=None, scratch=(), cost=1):
    out_specs = [VMEM] * len(shapes) if out_specs is None else out_specs
    return pl.pallas_call(
        kernel,
        in_specs=in_specs,
        out_specs=out_specs,
        out_shape=[jax.ShapeDtypeStruct(shape, dtype) for shape, dtype in shapes],
        scratch_shapes=list(scratch),
        compiler_params=PARAMS,
        cost_estimate=pl.CostEstimate(flops=cost, bytes_accessed=1, transcendentals=0),
        name=name,
    )(*args)


def local(green, occupation, offsets, qtable, coupling, pattern):
    e_axes = ("em", "rep")
    x1, x2 = swap_pairs(lax.axis_size("blk"), 0), swap_pairs(lax.axis_size("blk"), 1)
    y_count = lax.axis_size(e_axes)
    y1, y2 = swap_pairs(y_count, 0), swap_pairs(y_count, 1)
    odd = lax.axis_index("rep") % 2
    tau1 = 1 - lax.axis_index("blk") % 2
    scalars = jnp.stack([tau1, 1 - tau1, odd]).astype(jnp.int32)
    second = green.shape[3] - FIRST
    dma = pltpu.SemaphoreType.DMA

    first2, whole1, second2 = call(
        edge_kernel,
        [SMEM, VMEM],
        [((2, 4, 2, rows, 256), BF16) for rows in (FIRST, FIRST + second, second)],
        (scalars, green),
        "edge",
    )
    first2 = lax.ppermute(first2, e_axes, y2)
    whole1 = lax.ppermute(whole1, e_axes, y1)
    second2 = lax.ppermute(second2, e_axes, y2)

    (weights,) = call(
        weight_kernel,
        [SMEM] * 4,
        [((256, 512), BF16)],
        (scalars, occupation, offsets, qtable),
        "weights",
    )
    eff = coupling * pattern[:, :, None, None].astype(BF16)

    def own(row, rows, side2, name):
        def kernel(*refs):
            own_kernel(row, *refs)

        return call(
            kernel,
            [SMEM] + [VMEM] * 4,
            [((4, 4, rows, 256), BF16)] * 2,
            (scalars, weights, green, whole1, side2),
            name,
        )

    own_first1, own_first2 = own(0, FIRST, first2, "own_first")
    rim_first2 = lax.ppermute(own_first2, "blk", x2)
    rim_first1 = lax.ppermute(own_first1, "blk", x1)
    own_second1, own_second2 = own(FIRST, second, second2, "own_second")
    rim_second2 = lax.ppermute(own_second2, "blk", x2)
    rim_second1 = lax.ppermute(own_second1, "blk", x1)
    (inner,) = call(
        inner_kernel,
        [SMEM] + [VMEM] * 5,
        [((4, 4, 2, 128, 256), jnp.float32)],
        (scalars, eff, own_first1, own_second1, own_first2, own_second2),
        "inner",
        scratch=[pltpu.VMEM((2, 16, 256, 256), BF16)],
    )
    (half,) = call(
        half_kernel,
        [SMEM] + [VMEM] * 3,
        [((2, 16, FIRST, 256), BF16)],
        (scalars, eff, rim_first1, rim_first2),
        "half",
    )
    (sigma,) = call(
        final_kernel,
        [SMEM] + [VMEM] * 5,
        [(green.shape, BF16)],
        (scalars, eff, inner, half, rim_second1, rim_second2),
        "final",
        out_specs=[ANY],
        scratch=[
            pltpu.VMEM((2, 16, second, 256), BF16),
            pltpu.VMEM(green.shape, BF16),
            dma((4,)),
        ],
    )
    return sigma


def solution(mesh):
    in_specs = (
        P(("em", "rep"), None, "blk", None, None),
        P(),
        P(),
        P(),
        P("blk", None, None, None),
        P("blk", None),
    )
    out_specs = P(("em", "rep"), None, "blk", None, None)
    return jax.shard_map(local, mesh=mesh, in_specs=in_specs, out_specs=out_specs, check_vma=False)
```

time: 77 us -> 50.5 us (0.66)
  the two profiles are of different devices: /device:TPU:509 before, /device:TPU:5 now
where the time goes in v1:
time: 50.5 us; the launch traced here: 50.2 us
  starting transfers between devices  25.8 us (51%)
  waiting for transfers between devices  12.4 us (25%)
  Pallas kernels  10 us (20%)
  local copies, waits for them, and re-layouts  1.62 us (3%)
    ppermute x1, starting transfers between devices, local(): rim_first2 = lax.ppermute(own_first2, 'blk', x2)  10.5 us
    pallas_call x7, Pallas kernels, call(): pl.pallas_call(kernel, in_specs=in_specs, out_specs=out_specs, out_shape=...  10 us
    ppermute x1, waiting for transfers between devices, local(): rim_second2 = lax.ppermute(own_second2, 'blk', x2)  4.63 us
    ppermute x1, waiting for transfers between devices, local(): first2 = lax.ppermute(first2, e_axes, y2)  4.48 us
    ppermute x1, waiting for transfers between devices, local(): rim_first2 = lax.ppermute(own_first2, 'blk', x2)  3.33 us
    ppermute x1, starting transfers between devices, local(): first2 = lax.ppermute(first2, e_axes, y2)  3.1 us
    ppermute x1, starting transfers between devices, local(): rim_first1 = lax.ppermute(own_first1, 'blk', x1)  2.96 us
    ppermute x1, starting transfers between devices, local(): whole1 = lax.ppermute(whole1, e_axes, y1)  2.58 us
  transfers between devices with their start and end apart: 7, of which 3 were waited for; matrix products, arithmetic and copies ran while one was open for 0% of the time, Pallas kernels for 14%

profile of v1, /device:TPU:5, one launch (start us, length us, event | category | flops | bytes accessed | tf_op | source)
XLA Modules:
  0.0 50.2 jit_solution(2447555842646204951)
XLA Ops:
  0.0 0.1 pad_add_fusion.s_ref.refs_0_
  0.1 1.6 %copy-done = bf16[4,4,2,128,256]{4,3,2,1,0:T(8,128)(2,1)S(1)} copy-done((bf16[4,4,2,128,256]{4,3,2,1,0:T(8,128)(2,1)S(1)}, bf16[4,4,2,128,256]{4,3,2,1,0:T(8,128)(2,1)}, u32[]{:S(2)}) %copy-start) | copy-done | bytes 2097176
  1.7 0.7 %edge.1 = (bf16[2,4,2,64,256]{4,3,2,1,0:T(8,128)(2,1)S(1)}, bf16[2,4,2,128,256]{4,3,2,1,0:T(8,128)(2,1)S(1)}, bf16[2,4,2,64,256]{4,3,2,1,0:T(8,128)(2,1)S(1)}) custom-call(s32[3]{0:T(128)S(1)} %pad_add_fusion.s_ref.refs_0_, bf16[4,4,2,128,256]{4,3,2,1,0:T(8,128)(2,1)S(1)} %copy-done), custom_call_target="tpu_custom_call" | custom-call | flops 1 | bytes 1 | tf_op jit(solution)/shard_map/edge/pallas_call | solution.py:165
  2.4 2.6 %collective-permute-start = (bf16[2,4,2,128,256]{4,3,2,1,0:T(8,128)(2,1)S(1)}, bf16[2,4,2,128,256]{4,3,2,1,0:T(8,128)(2,1)S(1)}, u32[]{:S(2)}, u32[]{:S(2)}) collective-permute-start(bf16[2,4,2,128,256]{4,3,2,1,0:T(8,128)(2,1)S(1)} %get-tuple-element.12), channel_id=1, source_target_pairs={{0,1},{2,3},{4,5},{6,7},{8,9},{10,11},{12,13},{14,15},{64,65},{66,... | collective-permute-start | bytes 3145736 | tf_op jit(solution)/shard_map/ppermute | solution.py:196
  5.0 3.1 %collective-permute-start.1 = (bf16[2,4,2,64,256]{4,3,2,1,0:T(8,128)(2,1)S(1)}, bf16[2,4,2,64,256]{4,3,2,1,0:T(8,128)(2,1)S(1)}, u32[]{:S(2)}, u32[]{:S(2)}) collective-permute-start(bf16[2,4,2,64,256]{4,3,2,1,0:T(8,128)(2,1)S(1)} %get-tuple-element.13), channel_id=1, source_target_pairs={{1,2},{3,4},{5,6},{7,8},{9,10},{11,12},{13,14},{15,64},{65,66},{67... | collective-permute-start | bytes 1572872 | tf_op jit(solution)/shard_map/ppermute | solution.py:195
  8.1 2.5 %collective-permute-start.2 = (bf16[2,4,2,64,256]{4,3,2,1,0:T(8,128)(2,1)S(1)}, bf16[2,4,2,64,256]{4,3,2,1,0:T(8,128)(2,1)S(1)}, u32[]{:S(2)}, u32[]{:S(2)}) collective-permute-start(bf16[2,4,2,64,256]{4,3,2,1,0:T(8,128)(2,1)S(1)} %get-tuple-element.15), channel_id=1, source_target_pairs={{1,2},{3,4},{5,6},{7,8},{9,10},{11,12},{13,14},{15,64},{65,66},{67... | collective-permute-start | bytes 1572872 | tf_op jit(solution)/shard_map/ppermute | solution.py:197
  10.6 0.0 copy-done.2
  10.6 0.0 copy-done.4
  10.6 0.0 copy-done.3
  10.6 0.7 %weights.1.refs_1_ = bf16[256,512]{1,0:T(8,128)(2,1)S(1)} custom-call(s32[3]{0:T(128)S(1)} %pad_add_fusion.s_ref.refs_0_, f32[4]{0:T(128)S(1)} %copy-done.3, s32[4]{0:T(128)S(1)} %copy-done.4, s32[4,4]{1,0:T(4,128)S(1)} %copy-done.2), custom_call_target="tpu_custom_call" | custom-call | flops 1 | bytes 1 | tf_op jit(solution)/shard_map/weights/pallas_call | solution.py:165
  11.3 4.5 %collective-permute-done.1.refs_4_ = bf16[2,4,2,64,256]{4,3,2,1,0:T(8,128)(2,1)S(1)} collective-permute-done((bf16[2,4,2,64,256]{4,3,2,1,0:T(8,128)(2,1)S(1)}, bf16[2,4,2,64,256]{4,3,2,1,0:T(8,128)(2,1)S(1)}, u32[]{:S(2)}, u32[]{:S(2)}) %collective-permute-start.1) | collective-permute-done | bytes 524320 | tf_op jit(solution)/shard_map/ppermute | solution.py:195
  15.8 0.0 collective-permute-done.refs_3_
  15.8 0.0 copy-done.1
  15.8 1.2 %own_first.1 = (bf16[4,4,64,256]{3,2,1,0:T(8,128)(2,1)S(1)}, bf16[4,4,64,256]{3,2,1,0:T(8,128)(2,1)S(1)}) custom-call(s32[3]{0:T(128)S(1)} %pad_add_fusion.s_ref.refs_0_, bf16[256,512]{1,0:T(8,128)(2,1)S(1)} %weights.1.refs_1_, bf16[4,4,2,128,256]{4,3,2,1,0:T(8,128)(2,1)S(1)} %copy-done.1, bf16[2,4,2,128,256]{4,3,2,1,0:T(8,128)(2,1)S(1)} %collective-permute-done.refs_3_, ...), custom_call_target="tpu_custom_call" | custom-call | flops 1 | bytes 1 | tf_op jit(solution)/shard_map/own_first/pallas_call | solution.py:165
  17.0 0.0 copy-start.6
  17.1 0.0 copy-start.5
  17.1 3.0 %collective-permute-start.3 = (bf16[4,4,64,256]{3,2,1,0:T(8,128)(2,1)S(1)}, bf16[4,4,64,256]{3,2,1,0:T(8,128)(2,1)S(1)}, u32[]{:S(2)}, u32[]{:S(2)}) collective-permute-start(bf16[4,4,64,256]{3,2,1,0:T(8,128)(2,1)S(1)} %get-tuple-element.14.first1), channel_id=1, source_target_pairs={{0,16},{32,48},{16,0},{48,32},{1,17},{33,49},{17,1},{49,33},{2,18}... | collective-permute-start | bytes 1572872 | tf_op jit(solution)/shard_map/ppermute | solution.py:222
  20.0 10.5 %collective-permute-start.4 = (bf16[4,4,64,256]{3,2,1,0:T(8,128)(2,1)S(1)}, bf16[4,4,64,256]{3,2,1,0:T(8,128)(2,1)S(1)}, u32[]{:S(2)}, u32[]{:S(2)}) collective-permute-start(bf16[4,4,64,256]{3,2,1,0:T(8,128)(2,1)S(1)} %get-tuple-element.17.first2), channel_id=1, source_target_pairs={{16,32},{32,16},{17,33},{33,17},{18,34},{34,18},{19,35},{35,19},{2... | collective-permute-start | bytes 1572872 | tf_op jit(solution)/shard_map/ppermute | solution.py:221
  30.5 0.0 collective-permute-done.2.refs_4_
  30.5 1.3 %own_second.1 = (bf16[4,4,64,256]{3,2,1,0:T(8,128)(2,1)S(1)}, bf16[4,4,64,256]{3,2,1,0:T(8,128)(2,1)S(1)}) custom-call(s32[3]{0:T(128)S(1)} %pad_add_fusion.s_ref.refs_0_, bf16[256,512]{1,0:T(8,128)(2,1)S(1)} %weights.1.refs_1_, bf16[4,4,2,128,256]{4,3,2,1,0:T(8,128)(2,1)S(1)} %copy-done.1, bf16[2,4,2,128,256]{4,3,2,1,0:T(8,128)(2,1)S(1)} %collective-permute-done.refs_3_, ...), custom_call_target="tpu_custom_call" | custom-call | flops 1 | bytes 1 | tf_op jit(solution)/shard_map/own_second/pallas_call | solution.py:165
  31.8 1.9 %collective-permute-start.5 = (bf16[4,4,64,256]{3,2,1,0:T(8,128)(2,1)S(1)}, bf16[4,4,64,256]{3,2,1,0:T(8,128)(2,1)S(1)}, u32[]{:S(2)}, u32[]{:S(2)}) collective-permute-start(bf16[4,4,64,256]{3,2,1,0:T(8,128)(2,1)S(1)} %get-tuple-element.16.second1), channel_id=1, source_target_pairs={{0,16},{32,48},{16,0},{48,32},{1,17},{33,49},{17,1},{49,33},{2,18}... | collective-permute-start | bytes 1572872 | tf_op jit(solution)/shard_map/ppermute | solution.py:225
  33.7 2.2 %collective-permute-start.6 = (bf16[4,4,64,256]{3,2,1,0:T(8,128)(2,1)S(1)}, bf16[4,4,64,256]{3,2,1,0:T(8,128)(2,1)S(1)}, u32[]{:S(2)}, u32[]{:S(2)}) collective-permute-start(bf16[4,4,64,256]{3,2,1,0:T(8,128)(2,1)S(1)} %get-tuple-element.18.second2), channel_id=1, source_target_pairs={{16,32},{32,16},{17,33},{33,17},{18,34},{34,18},{19,35},{35,19},{2... | collective-permute-start | bytes 1572872 | tf_op jit(solution)/shard_map/ppermute | solution.py:224
  36.0 0.0 copy-done.6
  36.0 0.0 copy-done.5
  36.0 0.1 broadcast_multiply_fusion.eff
  36.1 2.7 %inner.1 = f32[4,4,2,128,256]{4,3,2,1,0:T(8,128)S(1)} custom-call(s32[3]{0:T(128)S(1)} %pad_add_fusion.s_ref.refs_0_, bf16[2,3,128,128]{3,2,1,0:T(8,128)(2,1)S(1)} %broadcast_multiply_fusion.eff, bf16[4,4,64,256]{3,2,1,0:T(8,128)(2,1)S(1)} %get-tuple-element.14.first1, bf16[4,4,64,256]{3,2,1,0:T(8,128)(2,1)S(1)} %get-tuple-element.16.second1, ...), custom_call_target="tpu_custom_call" | custom-call | flops 1 | bytes 1 | tf_op jit(solution)/shard_map/inner/pallas_call | solution.py:165
  38.8 0.0 collective-permute-done.3.first1
  38.8 3.3 %collective-permute-done.4.first2 = bf16[4,4,64,256]{3,2,1,0:T(8,128)(2,1)S(1)} collective-permute-done((bf16[4,4,64,256]{3,2,1,0:T(8,128)(2,1)S(1)}, bf16[4,4,64,256]{3,2,1,0:T(8,128)(2,1)S(1)}, u32[]{:S(2)}, u32[]{:S(2)}) %collective-permute-start.4) | collective-permute-done | bytes 524320 | tf_op jit(solution)/shard_map/ppermute | solution.py:221
  42.1 1.0 %half.1 = bf16[2,16,64,256]{3,2,1,0:T(8,128)(2,1)S(1)} custom-call(s32[3]{0:T(128)S(1)} %pad_add_fusion.s_ref.refs_0_, bf16[2,3,128,128]{3,2,1,0:T(8,128)(2,1)S(1)} %broadcast_multiply_fusion.eff, bf16[4,4,64,256]{3,2,1,0:T(8,128)(2,1)S(1)} %collective-permute-done.3.first1, bf16[4,4,64,256]{3,2,1,0:T(8,128)(2,1)S(1)} %collective-permute-done.4.first2), custom_call_target="tpu_custom_call" | custom-call | flops 1 | bytes 1 | tf_op jit(solution)/shard_map/half/pallas_call | solution.py:165
  43.1 0.0 collective-permute-done.5.second1
  43.1 4.6 %collective-permute-done.6.second2 = bf16[4,4,64,256]{3,2,1,0:T(8,128)(2,1)S(1)} collective-permute-done((bf16[4,4,64,256]{3,2,1,0:T(8,128)(2,1)S(1)}, bf16[4,4,64,256]{3,2,1,0:T(8,128)(2,1)S(1)}, u32[]{:S(2)}, u32[]{:S(2)}) %collective-permute-start.6) | collective-permute-done | bytes 524320 | tf_op jit(solution)/shard_map/ppermute | solution.py:224
  47.8 2.5 %final.1 = bf16[4,4,2,128,256]{4,3,2,1,0:T(8,128)(2,1)} custom-call(s32[3]{0:T(128)S(1)} %pad_add_fusion.s_ref.refs_0_, bf16[2,3,128,128]{3,2,1,0:T(8,128)(2,1)S(1)} %broadcast_multiply_fusion.eff, f32[4,4,2,128,256]{4,3,2,1,0:T(8,128)S(1)} %inner.1, bf16[2,16,64,256]{3,2,1,0:T(8,128)(2,1)S(1)} %half.1, ...), custom_call_target="tpu_custom_call" | custom-call | flops 1 | bytes 1 | tf_op jit(solution)/shard_map/final/pallas_call | solution.py:165
  (6 shorter events, 0.0 us)
Async XLA Ops:
  0.0 10.6 %copy-start.2 = (s32[4,4]{1,0:T(4,128)S(1)}, s32[4,4]{1,0:T(4,128)}, u32[]{:S(2)}) copy-start(s32[4,4]{1,0:T(4,128)} %qtable.1) | copy-start | bytes 196
  0.0 10.6 %copy-start.4 = (s32[4]{0:T(128)S(1)}, s32[4]{0:T(128)}, u32[]{:S(2)}) copy-start(s32[4]{0:T(128)} %offsets.1) | copy-start | bytes 52
  0.0 10.6 %copy-start.3 = (f32[4]{0:T(128)S(1)}, f32[4]{0:T(128)}, u32[]{:S(2)}) copy-start(f32[4]{0:T(128)} %occupation.1) | copy-start | bytes 52
  0.1 1.6 %copy-start = (bf16[4,4,2,128,256]{4,3,2,1,0:T(8,128)(2,1)S(1)}, bf16[4,4,2,128,256]{4,3,2,1,0:T(8,128)(2,1)}, u32[]{:S(2)}) copy-start(bf16[4,4,2,128,256]{4,3,2,1,0:T(8,128)(2,1)} %refs_2_.3) | copy-start | bytes 6291460
  1.7 14.1 %copy-start.1 = (bf16[4,4,2,128,256]{4,3,2,1,0:T(8,128)(2,1)S(1)}, bf16[4,4,2,128,256]{4,3,2,1,0:T(8,128)(2,1)}, u32[]{:S(2)}) copy-start(bf16[4,4,2,128,256]{4,3,2,1,0:T(8,128)(2,1)} %refs_2_.3) | copy-start | bytes 6291460
  2.4 13.4 %collective-permute-start = (bf16[2,4,2,128,256]{4,3,2,1,0:T(8,128)(2,1)S(1)}, bf16[2,4,2,128,256]{4,3,2,1,0:T(8,128)(2,1)S(1)}, u32[]{:S(2)}, u32[]{:S(2)}) collective-permute-start(bf16[2,4,2,128,256]{4,3,2,1,0:T(8,128)(2,1)S(1)} %get-tuple-element.12), channel_id=1, source_target_pairs={{0,1},{2,3},{4,5},{6,7},{8,9},{10,11},{12,13},{14,15},{64,65},{66,... | collective-permute-start | bytes 3145736 | tf_op jit(solution)/shard_map/ppermute | solution.py:196
  5.0 10.8 %collective-permute-start.1 = (bf16[2,4,2,64,256]{4,3,2,1,0:T(8,128)(2,1)S(1)}, bf16[2,4,2,64,256]{4,3,2,1,0:T(8,128)(2,1)S(1)}, u32[]{:S(2)}, u32[]{:S(2)}) collective-permute-start(bf16[2,4,2,64,256]{4,3,2,1,0:T(8,128)(2,1)S(1)} %get-tuple-element.13), channel_id=1, source_target_pairs={{1,2},{3,4},{5,6},{7,8},{9,10},{11,12},{13,14},{15,64},{65,66},{67... | collective-permute-start | bytes 1572872 | tf_op jit(solution)/shard_map/ppermute | solution.py:195
  8.1 22.4 %collective-permute-start.2 = (bf16[2,4,2,64,256]{4,3,2,1,0:T(8,128)(2,1)S(1)}, bf16[2,4,2,64,256]{4,3,2,1,0:T(8,128)(2,1)S(1)}, u32[]{:S(2)}, u32[]{:S(2)}) collective-permute-start(bf16[2,4,2,64,256]{4,3,2,1,0:T(8,128)(2,1)S(1)} %get-tuple-element.15), channel_id=1, source_target_pairs={{1,2},{3,4},{5,6},{7,8},{9,10},{11,12},{13,14},{15,64},{65,66},{67... | collective-permute-start | bytes 1572872 | tf_op jit(solution)/shard_map/ppermute | solution.py:197
  17.0 18.9 %copy-start.6 = (s32[2,3]{1,0:T(2,128)S(1)}, s32[2,3]{1,0:T(2,128)}, u32[]{:S(2)}) copy-start(s32[2,3]{1,0:T(2,128)} %param.11) | copy-start | bytes 76
  17.1 19.0 %copy-start.5 = (bf16[2,3,128,128]{3,2,1,0:T(8,128)(2,1)S(1)}, bf16[2,3,128,128]{3,2,1,0:T(8,128)(2,1)}, u32[]{:S(2)}) copy-start(bf16[2,3,128,128]{3,2,1,0:T(8,128)(2,1)} %param.10) | copy-start | bytes 589828
  17.1 21.7 %collective-permute-start.3 = (bf16[4,4,64,256]{3,2,1,0:T(8,128)(2,1)S(1)}, bf16[4,4,64,256]{3,2,1,0:T(8,128)(2,1)S(1)}, u32[]{:S(2)}, u32[]{:S(2)}) collective-permute-start(bf16[4,4,64,256]{3,2,1,0:T(8,128)(2,1)S(1)} %get-tuple-element.14.first1), channel_id=1, source_target_pairs={{0,16},{32,48},{16,0},{48,32},{1,17},{33,49},{17,1},{49,33},{2,18}... | collective-permute-start | bytes 1572872 | tf_op jit(solution)/shard_map/ppermute | solution.py:222
  20.0 22.1 %collective-permute-start.4 = (bf16[4,4,64,256]{3,2,1,0:T(8,128)(2,1)S(1)}, bf16[4,4,64,256]{3,2,1,0:T(8,128)(2,1)S(1)}, u32[]{:S(2)}, u32[]{:S(2)}) collective-permute-start(bf16[4,4,64,256]{3,2,1,0:T(8,128)(2,1)S(1)} %get-tuple-element.17.first2), channel_id=1, source_target_pairs={{16,32},{32,16},{17,33},{33,17},{18,34},{34,18},{19,35},{35,19},{2... | collective-permute-start | bytes 1572872 | tf_op jit(solution)/shard_map/ppermute | solution.py:221
  31.8 11.3 %collective-permute-start.5 = (bf16[4,4,64,256]{3,2,1,0:T(8,128)(2,1)S(1)}, bf16[4,4,64,256]{3,2,1,0:T(8,128)(2,1)S(1)}, u32[]{:S(2)}, u32[]{:S(2)}) collective-permute-start(bf16[4,4,64,256]{3,2,1,0:T(8,128)(2,1)S(1)} %get-tuple-element.16.second1), channel_id=1, source_target_pairs={{0,16},{32,48},{16,0},{48,32},{1,17},{33,49},{17,1},{49,33},{2,18}... | collective-permute-start | bytes 1572872 | tf_op jit(solution)/shard_map/ppermute | solution.py:225
  33.7 14.0 %collective-permute-start.6 = (bf16[4,4,64,256]{3,2,1,0:T(8,128)(2,1)S(1)}, bf16[4,4,64,256]{3,2,1,0:T(8,128)(2,1)S(1)}, u32[]{:S(2)}, u32[]{:S(2)}) collective-permute-start(bf16[4,4,64,256]{3,2,1,0:T(8,128)(2,1)S(1)} %get-tuple-element.18.second2), channel_id=1, source_target_pairs={{16,32},{32,16},{17,33},{33,17},{18,34},{34,18},{19,35},{35,19},{2... | collective-permute-start | bytes 1572872 | tf_op jit(solution)/shard_map/ppermute | solution.py:224

commit v2 on v1

--- a/solution.py
+++ b/solution.py
@@ -6,9 +6,10 @@
 from jax.sharding import PartitionSpec as P
 
 REACH = 2
-FIRST = 64
+RAW = 64
 VMEM = pl.BlockSpec(memory_space=pltpu.VMEM)
 SMEM = pl.BlockSpec(memory_space=pltpu.SMEM)
+HBM = pl.BlockSpec(memory_space=pltpu.HBM)
 ANY = pl.BlockSpec(memory_space=pl.ANY)
 PARAMS = pltpu.CompilerParams(vmem_limit_bytes=40 * 2**20)
 BF16 = jnp.bfloat16
@@ -19,13 +20,27 @@
     return pairs + [(b, a) for a, b in pairs]
 
 
-def edge_kernel(s_ref, green, first2, whole1, second2):
-    rows = first2.shape[3]
+def load_kernel(s_ref, green, raw2, raw1, late2, whole1, early2):
+    raw = early2.shape[3]
     one, two = 2 - 2 * s_ref[2], 2 * s_ref[2]
+    for e in range(4):
+        raw2[e] = green[e, :, s_ref[1], :raw]
+        raw1[e] = green[e, :, s_ref[0], :raw]
     for e in range(REACH):
-        first2[e] = green[two + e, :, :, :rows]
+        late2[e] = green[two + e, :, :, raw:]
         whole1[e] = green[one + e]
-        second2[e] = green[two + e, :, :, rows:]
+        early2[e] = green[two + e, :, :, :raw]
+
+
+def far_kernel(s_ref, raw2, raw1, after, far2, far1):
+    del after
+    one, two = 2 - 2 * s_ref[2], 2 * s_ref[2]
+    for slot, raw in enumerate((raw1, raw2)):
+        for e in range(REACH):
+            for l in range(4):
+                far2[8 * e + 2 * l + slot] = raw[two + e, l]
+                far1[8 * e + 2 * l + slot] = raw[one + e, l]
+    far2[16] = jnp.zeros(far2.shape[1:], BF16)
 
 
 def weight_kernel(s_ref, occupation, offsets, qtable, out):
@@ -74,7 +89,8 @@
             out[e, k, pl.ds(out_row, 16)] = total[n : n + 16]
 
 
-def own_kernel(row, s_ref, weights, green, side1, side2, out1, out2):
+def own_kernel(row, side1_row, s_ref, weights, green, side1, after, side2, out1, out2):
+    del after
     for slot, out in ((0, out1), (1, out2)):
         tile = s_ref[slot]
 
@@ -82,7 +98,7 @@
             r = pl.multiple_of(n * 16, 16)
             aggregate_rows(
                 weights,
-                lambda e, l: side1[e, l, tile, pl.ds(r + row, 16)],
+                lambda e, l: side1[e, l, tile, pl.ds(r + side1_row, 16)],
                 lambda e, l: green[e, l, tile, pl.ds(r + row, 16)],
                 lambda e, l: side2[e, l, tile, pl.ds(r, 16)],
                 out,
@@ -103,14 +119,14 @@
     return u.astype(BF16).reshape(16, rows, weight.shape[0])
 
 
-def inner_kernel(s_ref, eff, first1, second1, first2, second2, out, work):
+def inner_kernel(s_ref, eff, late1, late2, early1, early2, out, work):
     tau = [s_ref[0], s_ref[1]]
     pair = [
         jnp.concatenate([eff[tau[0], 1], eff[tau[1], 2 - 2 * tau[1]]], axis=0),
         jnp.concatenate([eff[tau[0], 2 - 2 * tau[0]], eff[tau[1], 1]], axis=0),
     ]
-    raw = first1.shape[2]
-    for source, parts in enumerate(((first1, second1), (first2, second2))):
+    raw = early1.shape[2]
+    for source, parts in enumerate(((early1, late1), (early2, late2))):
         for part, row in zip(parts, (0, raw)):
             for p in range(2):
                 u = right_products(part, pair[source], p)
@@ -133,25 +149,42 @@
     lax.fori_loop(0, 4, step, 0, unroll=2)
 
 
-def half_kernel(s_ref, eff, first1, first2, out):
-    for a, part in enumerate((first1, first2)):
+def late_kernel(s_ref, eff, late2, late1, out):
+    for a, part in enumerate((late1, late2)):
         rim = eff[s_ref[a], 2 * s_ref[a]]
         for p in range(2):
             out[a, :, :, p * 128 : (p + 1) * 128] = right_products(part, rim, p)
 
 
-def final_kernel(s_ref, eff, inner, half, second1, second2, out, work, store, sems):
+def final_kernel(
+    s_ref, eff, inner, late, weights, raw1, raw2, far1, far2, out, early1, early2, work, store, sems
+):
     tau = [s_ref[0], s_ref[1]]
     rim = [eff[tau[a], 2 * tau[a]] for a in range(2)]
-    for a, part in enumerate((second1, second2)):
+    rows = raw1.shape[2]
+    for a, (raw, early) in enumerate(((raw1, early1), (raw2, early2))):
+
+        def step(n, carry):
+            r = pl.multiple_of(n * 16, 16)
+            aggregate_rows(
+                weights,
+                lambda e, l: far1[8 * e + 2 * l + a, pl.ds(r, 16)],
+                lambda e, l: raw[e, l, pl.ds(r, 16)],
+                lambda e, l: far2[8 * e + 2 * l + a, pl.ds(r, 16)],
+                early,
+                r,
+            )
+            return carry
+
+        lax.fori_loop(0, rows // 16, step, 0, unroll=4)
         for p in range(2):
-            work[a, :, :, p * 128 : (p + 1) * 128] = right_products(part, rim[a], p)
+            work[a, :, :, p * 128 : (p + 1) * 128] = right_products(early, rim[a], p)
 
     copies = []
     for e in range(4):
         for k in range(4):
             for a in range(2):
-                right = jnp.concatenate([half[a, 4 * e + k], work[a, 4 * e + k]], axis=0)
+                right = jnp.concatenate([work[a, 4 * e + k], late[a, 4 * e + k]], axis=0)
                 total = jnp.dot(rim[a], right, preferred_element_type=jnp.float32)
                 store[e, k, tau[a]] = (inner[e, k, a] + total).astype(BF16)
         copies.append(pltpu.make_async_copy(store.at[e], out.at[e], sems.at[e]))
@@ -182,19 +215,23 @@
     odd = lax.axis_index("rep") % 2
     tau1 = 1 - lax.axis_index("blk") % 2
     scalars = jnp.stack([tau1, 1 - tau1, odd]).astype(jnp.int32)
-    second = green.shape[3] - FIRST
+    late = green.shape[3] - RAW
     dma = pltpu.SemaphoreType.DMA
-
-    first2, whole1, second2 = call(
-        edge_kernel,
+    tile_raw, tile_late = ((4, 4, RAW, 256), BF16), ((4, 4, late, 256), BF16)
+
+    raw2, raw1, late2, whole1, early2 = call(
+        load_kernel,
         [SMEM, VMEM],
-        [((2, 4, 2, rows, 256), BF16) for rows in (FIRST, FIRST + second, second)],
+        [tile_raw, tile_raw]
+        + [((2, 4, 2, rows, 256), BF16) for rows in (late, late + RAW, RAW)],
         (scalars, green),
-        "edge",
-    )
-    first2 = lax.ppermute(first2, e_axes, y2)
+        "load",
+    )
+    raw2 = lax.ppermute(raw2, "blk", x2)
+    raw1 = lax.ppermute(raw1, "blk", x1)
+    late2 = lax.ppermute(late2, e_axes, y2)
     whole1 = lax.ppermute(whole1, e_axes, y1)
-    second2 = lax.ppermute(second2, e_axes, y2)
+    early2 = lax.ppermute(early2, e_axes, y2)
 
     (weights,) = call(
         weight_kernel,
@@ -202,51 +239,64 @@
         [((256, 512), BF16)],
         (scalars, occupation, offsets, qtable),
         "weights",
+        cost=10**11,
     )
     eff = coupling * pattern[:, :, None, None].astype(BF16)
 
-    def own(row, rows, side2, name):
+    def own(row, side1_row, side2, after, shape, name, cost=1):
         def kernel(*refs):
-            own_kernel(row, *refs)
+            own_kernel(row, side1_row, *refs)
 
         return call(
             kernel,
-            [SMEM] + [VMEM] * 4,
-            [((4, 4, rows, 256), BF16)] * 2,
-            (scalars, weights, green, whole1, side2),
+            [SMEM] + [VMEM] * 3 + [ANY, VMEM],
+            [shape] * 2,
+            (scalars, weights, green, whole1, after, side2),
             name,
+            cost=cost,
         )
 
-    own_first1, own_first2 = own(0, FIRST, first2, "own_first")
-    rim_first2 = lax.ppermute(own_first2, "blk", x2)
-    rim_first1 = lax.ppermute(own_first1, "blk", x1)
-    own_second1, own_second2 = own(FIRST, second, second2, "own_second")
-    rim_second2 = lax.ppermute(own_second2, "blk", x2)
-    rim_second1 = lax.ppermute(own_second1, "blk", x1)
+    own_late1, own_late2 = own(RAW, RAW, late2, whole1, tile_late, "own_late")
+    sent2, sent1 = call(
+        far_kernel,
+        [SMEM, VMEM, VMEM, ANY],
+        [((17, RAW, 256), BF16), ((16, RAW, 256), BF16)],
+        (scalars, raw2, raw1, own_late1),
+        "far",
+    )
+    rim_late2 = lax.ppermute(own_late2, "blk", x2)
+    rim_late1 = lax.ppermute(own_late1, "blk", x1)
+    far2 = lax.ppermute(sent2, e_axes, y2)
+    far1 = lax.ppermute(sent1, e_axes, y1)
+    own_early1, own_early2 = own(0, 0, early2, sent2, tile_raw, "own_early", 1)
     (inner,) = call(
         inner_kernel,
         [SMEM] + [VMEM] * 5,
         [((4, 4, 2, 128, 256), jnp.float32)],
-        (scalars, eff, own_first1, own_second1, own_first2, own_second2),
+        (scalars, eff, own_late1, own_late2, own_early1, own_early2),
         "inner",
+        cost=1,
         scratch=[pltpu.VMEM((2, 16, 256, 256), BF16)],
     )
-    (half,) = call(
-        half_kernel,
+    (rim_late,) = call(
+        late_kernel,
         [SMEM] + [VMEM] * 3,
-        [((2, 16, FIRST, 256), BF16)],
-        (scalars, eff, rim_first1, rim_first2),
-        "half",
+        [((2, 16, late, 256), BF16)],
+        (scalars, eff, rim_late2, rim_late1),
+        "late",
+        cost=1000000000,
     )
     (sigma,) = call(
         final_kernel,
-        [SMEM] + [VMEM] * 5,
+        [SMEM] + [VMEM] * 8,
         [(green.shape, BF16)],
-        (scalars, eff, inner, half, rim_second1, rim_second2),
+        (scalars, eff, inner, rim_late, weights, raw1, raw2, far1, far2),
         "final",
         out_specs=[ANY],
         scratch=[
-            pltpu.VMEM((2, 16, second, 256), BF16),
+            pltpu.VMEM((4, 4, RAW, 256), BF16),
+            pltpu.VMEM((4, 4, RAW, 256), BF16),
+            pltpu.VMEM((2, 16, RAW, 256), BF16),
             pltpu.VMEM(green.shape, BF16),
             dma((4,)),
         ],

time: 50.5 us -> 46.6 us (0.923)
  the two profiles are of different devices: /device:TPU:5 before, /device:TPU:512 now
where the time goes in v2:
time: 46.6 us; the launch traced here: 46.2 us
  starting transfers between devices  29.5 us (63%)
  Pallas kernels  11.4 us (24%)
  waiting for transfers between devices  3.27 us (7%)
  local copies, waits for them, and re-layouts  1.62 us (3%)
    pallas_call x8, Pallas kernels, call(): pl.pallas_call(kernel, in_specs=in_specs, out_specs=out_specs, out_shape=...  11.4 us
    ppermute x1, starting transfers between devices, local(): raw1 = lax.ppermute(raw1, 'blk', x1)  6.1 us
    ppermute x1, starting transfers between devices, local(): late2 = lax.ppermute(late2, e_axes, y2)  6.02 us
    ppermute x1, starting transfers between devices, local(): far2 = lax.ppermute(sent2, e_axes, y2)  5.74 us
    ppermute x1, starting transfers between devices, local(): rim_late1 = lax.ppermute(own_late1, 'blk', x1)  3.95 us
    ppermute x1, starting transfers between devices, local(): early2 = lax.ppermute(early2, e_axes, y2)  2.31 us
    ppermute x1, starting transfers between devices, local(): whole1 = lax.ppermute(whole1, e_axes, y1)  2.05 us
    ppermute x1, starting transfers between devices, local(): far1 = lax.ppermute(sent1, e_axes, y1)  1.92 us
  transfers between devices with their start and end apart: 9, of which 2 were waited for; matrix products, arithmetic and copies ran while one was open for 0% of the time, Pallas kernels for 16%

profile of v2, /device:TPU:512, one launch (start us, length us, event | category | flops | bytes accessed | tf_op | source)
XLA Modules:
  0.0 46.2 jit_solution(10149905693471089074)
XLA Ops:
  0.0 0.1 pad_add_fusion.s_ref.refs_0_
  0.1 1.6 %copy-done = bf16[4,4,2,128,256]{4,3,2,1,0:T(8,128)(2,1)S(1)} copy-done((bf16[4,4,2,128,256]{4,3,2,1,0:T(8,128)(2,1)S(1)}, bf16[4,4,2,128,256]{4,3,2,1,0:T(8,128)(2,1)}, u32[]{:S(2)}) %copy-start) | copy-done | bytes 2097176
  1.7 0.7 %load.1 = (bf16[4,4,64,256]{3,2,1,0:T(8,128)(2,1)S(1)}, bf16[4,4,64,256]{3,2,1,0:T(8,128)(2,1)S(1)}, bf16[2,4,2,64,256]{4,3,2,1,0:T(8,128)(2,1)S(1)}, bf16[2,4,2...) custom-call(s32[3]{0:T(128)S(1)} %pad_add_fusion.s_ref.refs_0_, bf16[4,4,2,128,256]{4,3,2,1,0:T(8,128)(2,1)S(1)} %copy-done), custom_call_target="tpu_custom_call" | custom-call | flops 1 | bytes 1 | tf_op jit(solution)/shard_map/load/pallas_call | solution.py:198
  2.5 6.0 %collective-permute-start.1 = (bf16[2,4,2,64,256]{4,3,2,1,0:T(8,128)(2,1)S(1)}, bf16[2,4,2,64,256]{4,3,2,1,0:T(8,128)(2,1)S(1)}, u32[]{:S(2)}, u32[]{:S(2)}) collective-permute-start(bf16[2,4,2,64,256]{4,3,2,1,0:T(8,128)(2,1)S(1)} %get-tuple-element.17), channel_id=1, source_target_pairs={{1,2},{3,4},{5,6},{7,8},{9,10},{11,12},{13,14},{15,64},{65,66},{67... | collective-permute-start | bytes 1572872 | tf_op jit(solution)/shard_map/ppermute | solution.py:232
  8.5 0.7 %collective-permute-start.2 = (bf16[4,4,64,256]{3,2,1,0:T(8,128)(2,1)S(1)}, bf16[4,4,64,256]{3,2,1,0:T(8,128)(2,1)S(1)}, u32[]{:S(2)}, u32[]{:S(2)}) collective-permute-start(bf16[4,4,64,256]{3,2,1,0:T(8,128)(2,1)S(1)} %get-tuple-element.20), channel_id=1, source_target_pairs={{16,32},{32,16},{17,33},{33,17},{18,34},{34,18},{19,35},{35,19},{2... | collective-permute-start | bytes 1572872 | tf_op jit(solution)/shard_map/ppermute | solution.py:230
  9.2 6.1 %collective-permute-start.3 = (bf16[4,4,64,256]{3,2,1,0:T(8,128)(2,1)S(1)}, bf16[4,4,64,256]{3,2,1,0:T(8,128)(2,1)S(1)}, u32[]{:S(2)}, u32[]{:S(2)}) collective-permute-start(bf16[4,4,64,256]{3,2,1,0:T(8,128)(2,1)S(1)} %get-tuple-element.21), channel_id=1, source_target_pairs={{0,16},{32,48},{16,0},{48,32},{1,17},{33,49},{17,1},{49,33},{2,18}... | collective-permute-start | bytes 1572872 | tf_op jit(solution)/shard_map/ppermute | solution.py:231
  15.3 2.3 %collective-permute-start.4 = (bf16[2,4,2,64,256]{4,3,2,1,0:T(8,128)(2,1)S(1)}, bf16[2,4,2,64,256]{4,3,2,1,0:T(8,128)(2,1)S(1)}, u32[]{:S(2)}, u32[]{:S(2)}) collective-permute-start(bf16[2,4,2,64,256]{4,3,2,1,0:T(8,128)(2,1)S(1)} %get-tuple-element.23), channel_id=1, source_target_pairs={{1,2},{3,4},{5,6},{7,8},{9,10},{11,12},{13,14},{15,64},{65,66},{67... | collective-permute-start | bytes 1572872 | tf_op jit(solution)/shard_map/ppermute | solution.py:234
  17.6 0.0 copy-start.1
  17.6 2.1 %collective-permute-start = (bf16[2,4,2,128,256]{4,3,2,1,0:T(8,128)(2,1)S(1)}, bf16[2,4,2,128,256]{4,3,2,1,0:T(8,128)(2,1)S(1)}, u32[]{:S(2)}, u32[]{:S(2)}) collective-permute-start(bf16[2,4,2,128,256]{4,3,2,1,0:T(8,128)(2,1)S(1)} %get-tuple-element.16), channel_id=1, source_target_pairs={{0,1},{2,3},{4,5},{6,7},{8,9},{10,11},{12,13},{14,15},{64,65},{66,... | collective-permute-start | bytes 3145736 | tf_op jit(solution)/shard_map/ppermute | solution.py:233
  19.7 0.7 %weights.1.refs_1_ = bf16[256,512]{1,0:T(8,128)(2,1)S(1)} custom-call(s32[3]{0:T(128)S(1)} %pad_add_fusion.s_ref.refs_0_, f32[4]{0:T(128)S(1)} %copy-done.3, s32[4]{0:T(128)S(1)} %copy-done.4, s32[4,4]{1,0:T(4,128)S(1)} %copy-done.2), custom_call_target="tpu_custom_call" | custom-call | flops 99999997952 | bytes 1 | tf_op jit(solution)/shard_map/weights/pallas_call | solution.py:198
  20.4 0.0 copy-start.6
  20.4 0.0 copy-start.5
  20.4 0.0 collective-permute-done.1.refs_5_
  20.5 1.9 %collective-permute-done.refs_3_.refs_4_ = bf16[2,4,2,128,256]{4,3,2,1,0:T(8,128)(2,1)S(1)} collective-permute-done((bf16[2,4,2,128,256]{4,3,2,1,0:T(8,128)(2,1)S(1)}, bf16[2,4,2,128,256]{4,3,2,1,0:T(8,128)(2,1)S(1)}, u32[]{:S(2)}, u32[]{:S(2)}) %collective-permute-start) | collective-permute-done | bytes 1048608 | tf_op jit(solution)/shard_map/ppermute | solution.py:233
  22.3 1.3 %own_late.1 = (bf16[4,4,64,256]{3,2,1,0:T(8,128)(2,1)S(1)}, bf16[4,4,64,256]{3,2,1,0:T(8,128)(2,1)S(1)}) custom-call(s32[3]{0:T(128)S(1)} %pad_add_fusion.s_ref.refs_0_, bf16[256,512]{1,0:T(8,128)(2,1)S(1)} %weights.1.refs_1_, bf16[4,4,2,128,256]{4,3,2,1,0:T(8,128)(2,1)S(1)} %copy-done.1, ...), custom_call_target="tpu_custom_call" | custom-call | flops 1 | bytes 1 | tf_op jit(solution)/shard_map/own_late/pallas_call | solution.py:198
  23.6 0.7 %collective-permute-start.5 = (bf16[4,4,64,256]{3,2,1,0:T(8,128)(2,1)S(1)}, bf16[4,4,64,256]{3,2,1,0:T(8,128)(2,1)S(1)}, u32[]{:S(2)}, u32[]{:S(2)}) collective-permute-start(bf16[4,4,64,256]{3,2,1,0:T(8,128)(2,1)S(1)} %get-tuple-element.19.late2), channel_id=1, source_target_pairs={{16,32},{32,16},{17,33},{33,17},{18,34},{34,18},{19,35},{35,19},{2... | collective-permute-start | bytes 1572872 | tf_op jit(solution)/shard_map/ppermute | solution.py:267
  24.3 4.0 %collective-permute-start.6 = (bf16[4,4,64,256]{3,2,1,0:T(8,128)(2,1)S(1)}, bf16[4,4,64,256]{3,2,1,0:T(8,128)(2,1)S(1)}, u32[]{:S(2)}, u32[]{:S(2)}) collective-permute-start(bf16[4,4,64,256]{3,2,1,0:T(8,128)(2,1)S(1)} %get-tuple-element.18.after.late1), channel_id=1, source_target_pairs={{0,16},{32,48},{16,0},{48,32},{1,17},{33,49},{17,1},{49,33},{2,18}... | collective-permute-start | bytes 1572872 | tf_op jit(solution)/shard_map/ppermute | solution.py:268
  28.2 0.0 collective-permute-done.2.raw2
  28.2 0.0 collective-permute-done.3.raw1
  28.3 0.6 %far.1 = (bf16[17,64,256]{2,1,0:T(8,128)(2,1)S(1)}, bf16[16,64,256]{2,1,0:T(8,128)(2,1)S(1)}) custom-call(s32[3]{0:T(128)S(1)} %pad_add_fusion.s_ref.refs_0_, bf16[4,4,64,256]{3,2,1,0:T(8,128)(2,1)S(1)} %collective-permute-done.2.raw2, bf16[4,4,64,256]{3,2,1,0:T(8,128)(2,1)S(1)} %collective-permute-done.3.raw1, ...), custom_call_target="tpu_custom_call" | custom-call | flops 1 | bytes 1 | tf_op jit(solution)/shard_map/far/pallas_call | solution.py:198
  28.9 5.7 %collective-permute-start.8 = (bf16[17,64,256]{2,1,0:T(8,128)(2,1)S(1)}, bf16[17,64,256]{2,1,0:T(8,128)(2,1)S(1)}, u32[]{:S(2)}, u32[]{:S(2)}) collective-permute-start(bf16[17,64,256]{2,1,0:T(8,128)(2,1)S(1)} %get-tuple-element.22.refs_4_), channel_id=1, source_target_pairs={{1,2},{3,4},{5,6},{7,8},{9,10},{11,12},{13,14},{15,64},{65,66},{67... | collective-permute-start | bytes 1671176 | tf_op jit(solution)/shard_map/ppermute | solution.py:269
  34.6 1.9 %collective-permute-start.7 = (bf16[16,64,256]{2,1,0:T(8,128)(2,1)S(1)}, bf16[16,64,256]{2,1,0:T(8,128)(2,1)S(1)}, u32[]{:S(2)}, u32[]{:S(2)}) collective-permute-start(bf16[16,64,256]{2,1,0:T(8,128)(2,1)S(1)} %get-tuple-element.26), channel_id=1, source_target_pairs={{0,1},{2,3},{4,5},{6,7},{8,9},{10,11},{12,13},{14,15},{64,65},{66,... | collective-permute-start | bytes 1572872 | tf_op jit(solution)/shard_map/ppermute | solution.py:270
  36.6 0.1 broadcast_multiply_fusion.eff
  36.7 0.0 collective-permute-done.4.refs_5_
  36.7 1.3 %own_early.1 = (bf16[4,4,64,256]{3,2,1,0:T(8,128)(2,1)S(1)}, bf16[4,4,64,256]{3,2,1,0:T(8,128)(2,1)S(1)}) custom-call(s32[3]{0:T(128)S(1)} %pad_add_fusion.s_ref.refs_0_, bf16[256,512]{1,0:T(8,128)(2,1)S(1)} %weights.1.refs_1_, bf16[4,4,2,128,256]{4,3,2,1,0:T(8,128)(2,1)S(1)} %copy-done.1, ...), custom_call_target="tpu_custom_call" | custom-call | flops 1 | bytes 1 | tf_op jit(solution)/shard_map/own_early/pallas_call | solution.py:198
  37.9 2.7 %inner.1 = f32[4,4,2,128,256]{4,3,2,1,0:T(8,128)S(1)} custom-call(s32[3]{0:T(128)S(1)} %pad_add_fusion.s_ref.refs_0_, bf16[2,3,128,128]{3,2,1,0:T(8,128)(2,1)S(1)} %broadcast_multiply_fusion.eff, bf16[4,4,64,256]{3,2,1,0:T(8,128)(2,1)S(1)} %get-tuple-element.18.after.late1, bf16[4,4,64,256]{3,2,1,0:T(8,128)(2,1)S(1)} %get-tuple-element.19.late2, ...), custom_call_target="tpu_custom_call" | custom-call | flops 1 | bytes 1 | tf_op jit(solution)/shard_map/inner/pallas_call | solution.py:198
  40.6 0.0 collective-permute-done.5.late2
  40.6 0.0 collective-permute-done.6.late1
  40.7 1.0 %late.1 = bf16[2,16,64,256]{3,2,1,0:T(8,128)(2,1)S(1)} custom-call(s32[3]{0:T(128)S(1)} %pad_add_fusion.s_ref.refs_0_, bf16[2,3,128,128]{3,2,1,0:T(8,128)(2,1)S(1)} %broadcast_multiply_fusion.eff, bf16[4,4,64,256]{3,2,1,0:T(8,128)(2,1)S(1)} %collective-permute-done.5.late2, bf16[4,4,64,256]{3,2,1,0:T(8,128)(2,1)S(1)} %collective-permute-done.6.late1), custom_call_target="tpu_custom_call" | custom-call | flops 1000000000 | bytes 1 | tf_op jit(solution)/shard_map/late/pallas_call | solution.py:198
  41.6 0.0 collective-permute-done.7.far1
  41.7 1.4 %collective-permute-done.8.far2 = bf16[17,64,256]{2,1,0:T(8,128)(2,1)S(1)} collective-permute-done((bf16[17,64,256]{2,1,0:T(8,128)(2,1)S(1)}, bf16[17,64,256]{2,1,0:T(8,128)(2,1)S(1)}, u32[]{:S(2)}, u32[]{:S(2)}) %collective-permute-start.8) | collective-permute-done | bytes 557088 | tf_op jit(solution)/shard_map/ppermute | solution.py:269
  43.0 3.2 %final.1 = bf16[4,4,2,128,256]{4,3,2,1,0:T(8,128)(2,1)} custom-call(s32[3]{0:T(128)S(1)} %pad_add_fusion.s_ref.refs_0_, bf16[2,3,128,128]{3,2,1,0:T(8,128)(2,1)S(1)} %broadcast_multiply_fusion.eff, f32[4,4,2,128,256]{4,3,2,1,0:T(8,128)S(1)} %inner.1, bf16[2,16,64,256]{3,2,1,0:T(8,128)(2,1)S(1)} %late.1, bf16[256,512]{1,0:T(8,128)(2,1)S(1)} %weights.1.refs_1_, ...), custom_call_target="tpu_custom_call" | custom-call | flops 1 | bytes 1 | tf_op jit(solution)/shard_map/final/pallas_call | solution.py:198
  (11 shorter events, 0.0 us)
Async XLA Ops:
  0.0 19.7 %copy-start.2 = (s32[4,4]{1,0:T(4,128)S(1)}, s32[4,4]{1,0:T(4,128)}, u32[]{:S(2)}) copy-start(s32[4,4]{1,0:T(4,128)} %qtable.1) | copy-start | bytes 196
  0.0 19.7 %copy-start.4 = (s32[4]{0:T(128)S(1)}, s32[4]{0:T(128)}, u32[]{:S(2)}) copy-start(s32[4]{0:T(128)} %offsets.1) | copy-start | bytes 52
  0.0 19.7 %copy-start.3 = (f32[4]{0:T(128)S(1)}, f32[4]{0:T(128)}, u32[]{:S(2)}) copy-start(f32[4]{0:T(128)} %occupation.1) | copy-start | bytes 52
  0.1 1.6 %copy-start = (bf16[4,4,2,128,256]{4,3,2,1,0:T(8,128)(2,1)S(1)}, bf16[4,4,2,128,256]{4,3,2,1,0:T(8,128)(2,1)}, u32[]{:S(2)}) copy-start(bf16[4,4,2,128,256]{4,3,2,1,0:T(8,128)(2,1)} %refs_2_.3) | copy-start | bytes 6291460
  2.5 18.0 %collective-permute-start.1 = (bf16[2,4,2,64,256]{4,3,2,1,0:T(8,128)(2,1)S(1)}, bf16[2,4,2,64,256]{4,3,2,1,0:T(8,128)(2,1)S(1)}, u32[]{:S(2)}, u32[]{:S(2)}) collective-permute-start(bf16[2,4,2,64,256]{4,3,2,1,0:T(8,128)(2,1)S(1)} %get-tuple-element.17), channel_id=1, source_target_pairs={{1,2},{3,4},{5,6},{7,8},{9,10},{11,12},{13,14},{15,64},{65,66},{67... | collective-permute-start | bytes 1572872 | tf_op jit(solution)/shard_map/ppermute | solution.py:232
  8.5 19.8 %collective-permute-start.2 = (bf16[4,4,64,256]{3,2,1,0:T(8,128)(2,1)S(1)}, bf16[4,4,64,256]{3,2,1,0:T(8,128)(2,1)S(1)}, u32[]{:S(2)}, u32[]{:S(2)}) collective-permute-start(bf16[4,4,64,256]{3,2,1,0:T(8,128)(2,1)S(1)} %get-tuple-element.20), channel_id=1, source_target_pairs={{16,32},{32,16},{17,33},{33,17},{18,34},{34,18},{19,35},{35,19},{2... | collective-permute-start | bytes 1572872 | tf_op jit(solution)/shard_map/ppermute | solution.py:230
  9.2 19.1 %collective-permute-start.3 = (bf16[4,4,64,256]{3,2,1,0:T(8,128)(2,1)S(1)}, bf16[4,4,64,256]{3,2,1,0:T(8,128)(2,1)S(1)}, u32[]{:S(2)}, u32[]{:S(2)}) collective-permute-start(bf16[4,4,64,256]{3,2,1,0:T(8,128)(2,1)S(1)} %get-tuple-element.21), channel_id=1, source_target_pairs={{0,16},{32,48},{16,0},{48,32},{1,17},{33,49},{17,1},{49,33},{2,18}... | collective-permute-start | bytes 1572872 | tf_op jit(solution)/shard_map/ppermute | solution.py:231
  15.3 21.4 %collective-permute-start.4 = (bf16[2,4,2,64,256]{4,3,2,1,0:T(8,128)(2,1)S(1)}, bf16[2,4,2,64,256]{4,3,2,1,0:T(8,128)(2,1)S(1)}, u32[]{:S(2)}, u32[]{:S(2)}) collective-permute-start(bf16[2,4,2,64,256]{4,3,2,1,0:T(8,128)(2,1)S(1)} %get-tuple-element.23), channel_id=1, source_target_pairs={{1,2},{3,4},{5,6},{7,8},{9,10},{11,12},{13,14},{15,64},{65,66},{67... | collective-permute-start | bytes 1572872 | tf_op jit(solution)/shard_map/ppermute | solution.py:234
  17.6 4.7 %copy-start.1 = (bf16[4,4,2,128,256]{4,3,2,1,0:T(8,128)(2,1)S(1)}, bf16[4,4,2,128,256]{4,3,2,1,0:T(8,128)(2,1)}, u32[]{:S(2)}) copy-start(bf16[4,4,2,128,256]{4,3,2,1,0:T(8,128)(2,1)} %refs_2_.3) | copy-start | bytes 6291460
  17.6 4.7 %collective-permute-start = (bf16[2,4,2,128,256]{4,3,2,1,0:T(8,128)(2,1)S(1)}, bf16[2,4,2,128,256]{4,3,2,1,0:T(8,128)(2,1)S(1)}, u32[]{:S(2)}, u32[]{:S(2)}) collective-permute-start(bf16[2,4,2,128,256]{4,3,2,1,0:T(8,128)(2,1)S(1)} %get-tuple-element.16), channel_id=1, source_target_pairs={{0,1},{2,3},{4,5},{6,7},{8,9},{10,11},{12,13},{14,15},{64,65},{66,... | collective-permute-start | bytes 3145736 | tf_op jit(solution)/shard_map/ppermute | solution.py:233
  20.4 16.1 %copy-start.6 = (s32[2,3]{1,0:T(2,128)S(1)}, s32[2,3]{1,0:T(2,128)}, u32[]{:S(2)}) copy-start(s32[2,3]{1,0:T(2,128)} %param.11) | copy-start | bytes 76
  20.4 16.1 %copy-start.5 = (bf16[2,3,128,128]{3,2,1,0:T(8,128)(2,1)S(1)}, bf16[2,3,128,128]{3,2,1,0:T(8,128)(2,1)}, u32[]{:S(2)}) copy-start(bf16[2,3,128,128]{3,2,1,0:T(8,128)(2,1)} %param.10) | copy-start | bytes 589828
  23.6 17.1 %collective-permute-start.5 = (bf16[4,4,64,256]{3,2,1,0:T(8,128)(2,1)S(1)}, bf16[4,4,64,256]{3,2,1,0:T(8,128)(2,1)S(1)}, u32[]{:S(2)}, u32[]{:S(2)}) collective-permute-start(bf16[4,4,64,256]{3,2,1,0:T(8,128)(2,1)S(1)} %get-tuple-element.19.late2), channel_id=1, source_target_pairs={{16,32},{32,16},{17,33},{33,17},{18,34},{34,18},{19,35},{35,19},{2... | collective-permute-start | bytes 1572872 | tf_op jit(solution)/shard_map/ppermute | solution.py:267
  24.3 16.4 %collective-permute-start.6 = (bf16[4,4,64,256]{3,2,1,0:T(8,128)(2,1)S(1)}, bf16[4,4,64,256]{3,2,1,0:T(8,128)(2,1)S(1)}, u32[]{:S(2)}, u32[]{:S(2)}) collective-permute-start(bf16[4,4,64,256]{3,2,1,0:T(8,128)(2,1)S(1)} %get-tuple-element.18.after.late1), channel_id=1, source_target_pairs={{0,16},{32,48},{16,0},{48,32},{1,17},{33,49},{17,1},{49,33},{2,18}... | collective-permute-start | bytes 1572872 | tf_op jit(solution)/shard_map/ppermute | solution.py:268
  28.9 14.2 %collective-permute-start.8 = (bf16[17,64,256]{2,1,0:T(8,128)(2,1)S(1)}, bf16[17,64,256]{2,1,0:T(8,128)(2,1)S(1)}, u32[]{:S(2)}, u32[]{:S(2)}) collective-permute-start(bf16[17,64,256]{2,1,0:T(8,128)(2,1)S(1)} %get-tuple-element.22.refs_4_), channel_id=1, source_target_pairs={{1,2},{3,4},{5,6},{7,8},{9,10},{11,12},{13,14},{15,64},{65,66},{67... | collective-permute-start | bytes 1671176 | tf_op jit(solution)/shard_map/ppermute | solution.py:269
  34.6 7.0 %collective-permute-start.7 = (bf16[16,64,256]{2,1,0:T(8,128)(2,1)S(1)}, bf16[16,64,256]{2,1,0:T(8,128)(2,1)S(1)}, u32[]{:S(2)}, u32[]{:S(2)}) collective-permute-start(bf16[16,64,256]{2,1,0:T(8,128)(2,1)S(1)} %get-tuple-element.26), channel_id=1, source_target_pairs={{0,1},{2,3},{4,5},{6,7},{8,9},{10,11},{12,13},{14,15},{64,65},{66,... | collective-permute-start | bytes 1572872 | tf_op jit(solution)/shard_map/ppermute | solution.py:270

commit v3 on v2

--- a/solution.py
+++ b/solution.py
@@ -43,7 +43,9 @@
     far2[16] = jnp.zeros(far2.shape[1:], BF16)
 
 
-def weight_kernel(s_ref, occupation, offsets, qtable, out):
+def weight_kernel(s_ref, occupation, offsets, qtable, early, out, early_out):
+    early_out[...] = early[...]
+
     def band(d):
         total = 0.0
         for s in range(4):
@@ -231,16 +233,16 @@
     raw1 = lax.ppermute(raw1, "blk", x1)
     late2 = lax.ppermute(late2, e_axes, y2)
     whole1 = lax.ppermute(whole1, e_axes, y1)
-    early2 = lax.ppermute(early2, e_axes, y2)
-
-    (weights,) = call(
+
+    weights, early2 = call(
         weight_kernel,
-        [SMEM] * 4,
-        [((256, 512), BF16)],
-        (scalars, occupation, offsets, qtable),
+        [SMEM] * 4 + [VMEM],
+        [((256, 512), BF16), (early2.shape, BF16)],
+        (scalars, occupation, offsets, qtable, early2),
         "weights",
         cost=10**11,
     )
+    early2 = lax.ppermute(early2, e_axes, y2)
     eff = coupling * pattern[:, :, None, None].astype(BF16)
 
     def own(row, side1_row, side2, after, shape, name, cost=1):

time: 46.6 us -> 45.4 us (0.974)
  waiting for transfers between devices: 3.27 us -> 2.19 us
    ppermute x1, waiting for transfers between devices: 1.85 us -> 0.01 us  [local(): whole1 = lax.ppermute(whole1, e_axes, y1)]
    ppermute x1, starting transfers between devices: 2.31 us -> 3.36 us  [local(): early2 = lax.ppermute(early2, e_axes, y2)]
    ppermute x1, waiting for transfers between devices: 1.4 us -> 2.17 us  [local(): far2 = lax.ppermute(sent2, e_axes, y2)]
    ppermute x1, starting transfers between devices: 5.74 us -> 4.96 us  [local(): far2 = lax.ppermute(sent2, e_axes, y2)]
  transfers between devices with their start and end apart: 9 -> 9, of which waited for: 2 -> 1; matrix products, arithmetic and copies ran while one was open for 0% -> 0% of each run, Pallas kernels for 16% -> 17%
where the time goes in v3:
time: 45.4 us; the launch traced here: 45.1 us
  starting transfers between devices  29.3 us (65%)
  Pallas kernels  11.4 us (25%)
  waiting for transfers between devices  2.19 us (5%)
  local copies, waits for them, and re-layouts  1.62 us (4%)
    pallas_call x8, Pallas kernels, call(): pl.pallas_call(kernel, in_specs=in_specs, out_specs=out_specs, out_shape=...  11.4 us
    ppermute x1, starting transfers between devices, local(): raw1 = lax.ppermute(raw1, 'blk', x1)  6.1 us
    ppermute x1, starting transfers between devices, local(): late2 = lax.ppermute(late2, e_axes, y2)  6.02 us
    ppermute x1, starting transfers between devices, local(): far2 = lax.ppermute(sent2, e_axes, y2)  4.96 us
    ppermute x1, starting transfers between devices, local(): rim_late1 = lax.ppermute(own_late1, 'blk', x1)  3.67 us
    ppermute x1, starting transfers between devices, local(): early2 = lax.ppermute(early2, e_axes, y2)  3.36 us
    ppermute x1, waiting for transfers between devices, local(): far2 = lax.ppermute(sent2, e_axes, y2)  2.17 us
    ppermute x1, starting transfers between devices, local(): whole1 = lax.ppermute(whole1, e_axes, y1)  1.92 us
  transfers between devices with their start and end apart: 9, of which 1 were waited for; matrix products, arithmetic and copies ran while one was open for 0% of the time, Pallas kernels for 17%

profile of v3, /device:TPU:512, one launch (start us, length us, event | category | flops | bytes accessed | tf_op | source)
XLA Modules:
  0.0 45.1 jit_solution(13027847947842035393)
XLA Ops:
  0.0 0.1 pad_add_fusion.s_ref.refs_0_
  0.1 1.6 %copy-done = bf16[4,4,2,128,256]{4,3,2,1,0:T(8,128)(2,1)S(1)} copy-done((bf16[4,4,2,128,256]{4,3,2,1,0:T(8,128)(2,1)S(1)}, bf16[4,4,2,128,256]{4,3,2,1,0:T(8,128)(2,1)}, u32[]{:S(2)}) %copy-start) | copy-done | bytes 2097176
  1.7 0.7 %load.1 = (bf16[4,4,64,256]{3,2,1,0:T(8,128)(2,1)S(1)}, bf16[4,4,64,256]{3,2,1,0:T(8,128)(2,1)S(1)}, bf16[2,4,2,64,256]{4,3,2,1,0:T(8,128)(2,1)S(1)}, bf16[2,4,2...) custom-call(s32[3]{0:T(128)S(1)} %pad_add_fusion.s_ref.refs_0_, bf16[4,4,2,128,256]{4,3,2,1,0:T(8,128)(2,1)S(1)} %copy-done), custom_call_target="tpu_custom_call" | custom-call | flops 1 | bytes 1 | tf_op jit(solution)/shard_map/load/pallas_call | solution.py:200
  2.5 6.0 %collective-permute-start.1 = (bf16[2,4,2,64,256]{4,3,2,1,0:T(8,128)(2,1)S(1)}, bf16[2,4,2,64,256]{4,3,2,1,0:T(8,128)(2,1)S(1)}, u32[]{:S(2)}, u32[]{:S(2)}) collective-permute-start(bf16[2,4,2,64,256]{4,3,2,1,0:T(8,128)(2,1)S(1)} %get-tuple-element.21), channel_id=1, source_target_pairs={{1,2},{3,4},{5,6},{7,8},{9,10},{11,12},{13,14},{15,64},{65,66},{67... | collective-permute-start | bytes 1572872 | tf_op jit(solution)/shard_map/ppermute | solution.py:234
  8.5 0.7 %collective-permute-start.2 = (bf16[4,4,64,256]{3,2,1,0:T(8,128)(2,1)S(1)}, bf16[4,4,64,256]{3,2,1,0:T(8,128)(2,1)S(1)}, u32[]{:S(2)}, u32[]{:S(2)}) collective-permute-start(bf16[4,4,64,256]{3,2,1,0:T(8,128)(2,1)S(1)} %get-tuple-element.24), channel_id=1, source_target_pairs={{16,32},{32,16},{17,33},{33,17},{18,34},{34,18},{19,35},{35,19},{2... | collective-permute-start | bytes 1572872 | tf_op jit(solution)/shard_map/ppermute | solution.py:232
  9.2 6.1 %collective-permute-start.3 = (bf16[4,4,64,256]{3,2,1,0:T(8,128)(2,1)S(1)}, bf16[4,4,64,256]{3,2,1,0:T(8,128)(2,1)S(1)}, u32[]{:S(2)}, u32[]{:S(2)}) collective-permute-start(bf16[4,4,64,256]{3,2,1,0:T(8,128)(2,1)S(1)} %get-tuple-element.25), channel_id=1, source_target_pairs={{0,16},{32,48},{16,0},{48,32},{1,17},{33,49},{17,1},{49,33},{2,18}... | collective-permute-start | bytes 1572872 | tf_op jit(solution)/shard_map/ppermute | solution.py:233
  15.3 1.9 %collective-permute-start = (bf16[2,4,2,128,256]{4,3,2,1,0:T(8,128)(2,1)S(1)}, bf16[2,4,2,128,256]{4,3,2,1,0:T(8,128)(2,1)S(1)}, u32[]{:S(2)}, u32[]{:S(2)}) collective-permute-start(bf16[2,4,2,128,256]{4,3,2,1,0:T(8,128)(2,1)S(1)} %get-tuple-element.20), channel_id=1, source_target_pairs={{0,1},{2,3},{4,5},{6,7},{8,9},{10,11},{12,13},{14,15},{64,65},{66,... | collective-permute-start | bytes 3145736 | tf_op jit(solution)/shard_map/ppermute | solution.py:235
  17.2 0.0 copy-start.1
  17.3 0.7 %weights.1 = (bf16[256,512]{1,0:T(8,128)(2,1)S(1)}, bf16[2,4,2,64,256]{4,3,2,1,0:T(8,128)(2,1)S(1)}) custom-call(s32[3]{0:T(128)S(1)} %pad_add_fusion.s_ref.refs_0_, f32[4]{0:T(128)S(1)} %copy-done.3, s32[4]{0:T(128)S(1)} %copy-done.4, s32[4,4]{1,0:T(4,128)S(1)} %copy-done.2, bf16[2,4,2,64,256]{4,3,2,1,0:T(8,128)(2,1)S(1)} %get-tuple-element.18.early), custom_call_target="tpu_custom_call" | custom-call | flops 99999997952 | bytes 1 | tf_op jit(solution)/shard_map/weights/pallas_call | solution.py:200
  18.0 3.4 %collective-permute-start.4 = (bf16[2,4,2,64,256]{4,3,2,1,0:T(8,128)(2,1)S(1)}, bf16[2,4,2,64,256]{4,3,2,1,0:T(8,128)(2,1)S(1)}, u32[]{:S(2)}, u32[]{:S(2)}) collective-permute-start(bf16[2,4,2,64,256]{4,3,2,1,0:T(8,128)(2,1)S(1)} %get-tuple-element.27), channel_id=1, source_target_pairs={{1,2},{3,4},{5,6},{7,8},{9,10},{11,12},{13,14},{15,64},{65,66},{67... | collective-permute-start | bytes 1572872 | tf_op jit(solution)/shard_map/ppermute | solution.py:245
  21.3 0.0 collective-permute-done.1.refs_5_
  21.4 0.0 collective-permute-done.refs_3_.refs_4_
  21.4 0.0 copy-start.6
  21.4 0.0 copy-start.5
  21.4 1.3 %own_late.1 = (bf16[4,4,64,256]{3,2,1,0:T(8,128)(2,1)S(1)}, bf16[4,4,64,256]{3,2,1,0:T(8,128)(2,1)S(1)}) custom-call(s32[3]{0:T(128)S(1)} %pad_add_fusion.s_ref.refs_0_, bf16[256,512]{1,0:T(8,128)(2,1)S(1)} %get-tuple-element.19.refs_1_.weights, bf16[4,4,2,128,256]{4,3,2,1,0:T(8,128)(2,1)S(1)} %copy-done.1, ...), custom_call_target="tpu_custom_call" | custom-call | flops 1 | bytes 1 | tf_op jit(solution)/shard_map/own_late/pallas_call | solution.py:200
  22.7 0.7 %collective-permute-start.5 = (bf16[4,4,64,256]{3,2,1,0:T(8,128)(2,1)S(1)}, bf16[4,4,64,256]{3,2,1,0:T(8,128)(2,1)S(1)}, u32[]{:S(2)}, u32[]{:S(2)}) collective-permute-start(bf16[4,4,64,256]{3,2,1,0:T(8,128)(2,1)S(1)} %get-tuple-element.23.late2), channel_id=1, source_target_pairs={{16,32},{32,16},{17,33},{33,17},{18,34},{34,18},{19,35},{35,19},{2... | collective-permute-start | bytes 1572872 | tf_op jit(solution)/shard_map/ppermute | solution.py:269
  23.4 3.7 %collective-permute-start.6 = (bf16[4,4,64,256]{3,2,1,0:T(8,128)(2,1)S(1)}, bf16[4,4,64,256]{3,2,1,0:T(8,128)(2,1)S(1)}, u32[]{:S(2)}, u32[]{:S(2)}) collective-permute-start(bf16[4,4,64,256]{3,2,1,0:T(8,128)(2,1)S(1)} %get-tuple-element.22.after.late1), channel_id=1, source_target_pairs={{0,16},{32,48},{16,0},{48,32},{1,17},{33,49},{17,1},{49,33},{2,18}... | collective-permute-start | bytes 1572872 | tf_op jit(solution)/shard_map/ppermute | solution.py:270
  27.0 0.0 collective-permute-done.2.raw2
  27.1 0.0 collective-permute-done.3.raw1
  27.1 0.6 %far.1 = (bf16[17,64,256]{2,1,0:T(8,128)(2,1)S(1)}, bf16[16,64,256]{2,1,0:T(8,128)(2,1)S(1)}) custom-call(s32[3]{0:T(128)S(1)} %pad_add_fusion.s_ref.refs_0_, bf16[4,4,64,256]{3,2,1,0:T(8,128)(2,1)S(1)} %collective-permute-done.2.raw2, bf16[4,4,64,256]{3,2,1,0:T(8,128)(2,1)S(1)} %collective-permute-done.3.raw1, ...), custom_call_target="tpu_custom_call" | custom-call | flops 1 | bytes 1 | tf_op jit(solution)/shard_map/far/pallas_call | solution.py:200
  27.7 5.0 %collective-permute-start.8 = (bf16[17,64,256]{2,1,0:T(8,128)(2,1)S(1)}, bf16[17,64,256]{2,1,0:T(8,128)(2,1)S(1)}, u32[]{:S(2)}, u32[]{:S(2)}) collective-permute-start(bf16[17,64,256]{2,1,0:T(8,128)(2,1)S(1)} %get-tuple-element.26.refs_4_), channel_id=1, source_target_pairs={{1,2},{3,4},{5,6},{7,8},{9,10},{11,12},{13,14},{15,64},{65,66},{67... | collective-permute-start | bytes 1671176 | tf_op jit(solution)/shard_map/ppermute | solution.py:271
  32.7 1.9 %collective-permute-start.7 = (bf16[16,64,256]{2,1,0:T(8,128)(2,1)S(1)}, bf16[16,64,256]{2,1,0:T(8,128)(2,1)S(1)}, u32[]{:S(2)}, u32[]{:S(2)}) collective-permute-start(bf16[16,64,256]{2,1,0:T(8,128)(2,1)S(1)} %get-tuple-element.30), channel_id=1, source_target_pairs={{0,1},{2,3},{4,5},{6,7},{8,9},{10,11},{12,13},{14,15},{64,65},{66,... | collective-permute-start | bytes 1572872 | tf_op jit(solution)/shard_map/ppermute | solution.py:272
  34.6 0.1 broadcast_multiply_fusion.eff
  34.7 0.0 collective-permute-done.4.refs_5_
  34.7 1.3 %own_early.1 = (bf16[4,4,64,256]{3,2,1,0:T(8,128)(2,1)S(1)}, bf16[4,4,64,256]{3,2,1,0:T(8,128)(2,1)S(1)}) custom-call(s32[3]{0:T(128)S(1)} %pad_add_fusion.s_ref.refs_0_, bf16[256,512]{1,0:T(8,128)(2,1)S(1)} %get-tuple-element.19.refs_1_.weights, bf16[4,4,2,128,256]{4,3,2,1,0:T(8,128)(2,1)S(1)} %copy-done.1, ...), custom_call_target="tpu_custom_call" | custom-call | flops 1 | bytes 1 | tf_op jit(solution)/shard_map/own_early/pallas_call | solution.py:200
  36.0 2.7 %inner.1 = f32[4,4,2,128,256]{4,3,2,1,0:T(8,128)S(1)} custom-call(s32[3]{0:T(128)S(1)} %pad_add_fusion.s_ref.refs_0_, bf16[2,3,128,128]{3,2,1,0:T(8,128)(2,1)S(1)} %broadcast_multiply_fusion.eff, bf16[4,4,64,256]{3,2,1,0:T(8,128)(2,1)S(1)} %get-tuple-element.22.after.late1, bf16[4,4,64,256]{3,2,1,0:T(8,128)(2,1)S(1)} %get-tuple-element.23.late2, ...), custom_call_target="tpu_custom_call" | custom-call | flops 1 | bytes 1 | tf_op jit(solution)/shard_map/inner/pallas_call | solution.py:200
  38.7 0.0 collective-permute-done.5.late2
  38.7 0.0 collective-permute-done.6.late1
  38.7 1.0 %late.1 = bf16[2,16,64,256]{3,2,1,0:T(8,128)(2,1)S(1)} custom-call(s32[3]{0:T(128)S(1)} %pad_add_fusion.s_ref.refs_0_, bf16[2,3,128,128]{3,2,1,0:T(8,128)(2,1)S(1)} %broadcast_multiply_fusion.eff, bf16[4,4,64,256]{3,2,1,0:T(8,128)(2,1)S(1)} %collective-permute-done.5.late2, bf16[4,4,64,256]{3,2,1,0:T(8,128)(2,1)S(1)} %collective-permute-done.6.late1), custom_call_target="tpu_custom_call" | custom-call | flops 1000000000 | bytes 1 | tf_op jit(solution)/shard_map/late/pallas_call | solution.py:200
  39.7 0.0 collective-permute-done.7.far1
  39.7 2.2 %collective-permute-done.8.far2 = bf16[17,64,256]{2,1,0:T(8,128)(2,1)S(1)} collective-permute-done((bf16[17,64,256]{2,1,0:T(8,128)(2,1)S(1)}, bf16[17,64,256]{2,1,0:T(8,128)(2,1)S(1)}, u32[]{:S(2)}, u32[]{:S(2)}) %collective-permute-start.8) | collective-permute-done | bytes 557088 | tf_op jit(solution)/shard_map/ppermute | solution.py:271
  41.9 3.2 %final.1 = bf16[4,4,2,128,256]{4,3,2,1,0:T(8,128)(2,1)} custom-call(s32[3]{0:T(128)S(1)} %pad_add_fusion.s_ref.refs_0_, bf16[2,3,128,128]{3,2,1,0:T(8,128)(2,1)S(1)} %broadcast_multiply_fusion.eff, f32[4,4,2,128,256]{4,3,2,1,0:T(8,128)S(1)} %inner.1, bf16[2,16,64,256]{3,2,1,0:T(8,128)(2,1)S(1)} %late.1, ...), custom_call_target="tpu_custom_call" | custom-call | flops 1 | bytes 1 | tf_op jit(solution)/shard_map/final/pallas_call | solution.py:200
  (11 shorter events, 0.0 us)
Async XLA Ops:
  0.0 17.2 %copy-start.2 = (s32[4,4]{1,0:T(4,128)S(1)}, s32[4,4]{1,0:T(4,128)}, u32[]{:S(2)}) copy-start(s32[4,4]{1,0:T(4,128)} %qtable.1) | copy-start | bytes 196
  0.0 17.2 %copy-start.4 = (s32[4]{0:T(128)S(1)}, s32[4]{0:T(128)}, u32[]{:S(2)}) copy-start(s32[4]{0:T(128)} %offsets.1) | copy-start | bytes 52
  0.0 17.2 %copy-start.3 = (f32[4]{0:T(128)S(1)}, f32[4]{0:T(128)}, u32[]{:S(2)}) copy-start(f32[4]{0:T(128)} %occupation.1) | copy-start | bytes 52
  0.1 1.6 %copy-start = (bf16[4,4,2,128,256]{4,3,2,1,0:T(8,128)(2,1)S(1)}, bf16[4,4,2,128,256]{4,3,2,1,0:T(8,128)(2,1)}, u32[]{:S(2)}) copy-start(bf16[4,4,2,128,256]{4,3,2,1,0:T(8,128)(2,1)} %refs_2_.3) | copy-start | bytes 6291460
  2.5 18.9 %collective-permute-start.1 = (bf16[2,4,2,64,256]{4,3,2,1,0:T(8,128)(2,1)S(1)}, bf16[2,4,2,64,256]{4,3,2,1,0:T(8,128)(2,1)S(1)}, u32[]{:S(2)}, u32[]{:S(2)}) collective-permute-start(bf16[2,4,2,64,256]{4,3,2,1,0:T(8,128)(2,1)S(1)} %get-tuple-element.21), channel_id=1, source_target_pairs={{1,2},{3,4},{5,6},{7,8},{9,10},{11,12},{13,14},{15,64},{65,66},{67... | collective-permute-start | bytes 1572872 | tf_op jit(solution)/shard_map/ppermute | solution.py:234
  8.5 18.6 %collective-permute-start.2 = (bf16[4,4,64,256]{3,2,1,0:T(8,128)(2,1)S(1)}, bf16[4,4,64,256]{3,2,1,0:T(8,128)(2,1)S(1)}, u32[]{:S(2)}, u32[]{:S(2)}) collective-permute-start(bf16[4,4,64,256]{3,2,1,0:T(8,128)(2,1)S(1)} %get-tuple-element.24), channel_id=1, source_target_pairs={{16,32},{32,16},{17,33},{33,17},{18,34},{34,18},{19,35},{35,19},{2... | collective-permute-start | bytes 1572872 | tf_op jit(solution)/shard_map/ppermute | solution.py:232
  9.2 17.9 %collective-permute-start.3 = (bf16[4,4,64,256]{3,2,1,0:T(8,128)(2,1)S(1)}, bf16[4,4,64,256]{3,2,1,0:T(8,128)(2,1)S(1)}, u32[]{:S(2)}, u32[]{:S(2)}) collective-permute-start(bf16[4,4,64,256]{3,2,1,0:T(8,128)(2,1)S(1)} %get-tuple-element.25), channel_id=1, source_target_pairs={{0,16},{32,48},{16,0},{48,32},{1,17},{33,49},{17,1},{49,33},{2,18}... | collective-permute-start | bytes 1572872 | tf_op jit(solution)/shard_map/ppermute | solution.py:233
  15.3 6.1 %collective-permute-start = (bf16[2,4,2,128,256]{4,3,2,1,0:T(8,128)(2,1)S(1)}, bf16[2,4,2,128,256]{4,3,2,1,0:T(8,128)(2,1)S(1)}, u32[]{:S(2)}, u32[]{:S(2)}) collective-permute-start(bf16[2,4,2,128,256]{4,3,2,1,0:T(8,128)(2,1)S(1)} %get-tuple-element.20), channel_id=1, source_target_pairs={{0,1},{2,3},{4,5},{6,7},{8,9},{10,11},{12,13},{14,15},{64,65},{66,... | collective-permute-start | bytes 3145736 | tf_op jit(solution)/shard_map/ppermute | solution.py:235
  17.2 4.1 %copy-start.1 = (bf16[4,4,2,128,256]{4,3,2,1,0:T(8,128)(2,1)S(1)}, bf16[4,4,2,128,256]{4,3,2,1,0:T(8,128)(2,1)}, u32[]{:S(2)}) copy-start(bf16[4,4,2,128,256]{4,3,2,1,0:T(8,128)(2,1)} %refs_2_.3) | copy-start | bytes 6291460
  18.0 16.7 %collective-permute-start.4 = (bf16[2,4,2,64,256]{4,3,2,1,0:T(8,128)(2,1)S(1)}, bf16[2,4,2,64,256]{4,3,2,1,0:T(8,128)(2,1)S(1)}, u32[]{:S(2)}, u32[]{:S(2)}) collective-permute-start(bf16[2,4,2,64,256]{4,3,2,1,0:T(8,128)(2,1)S(1)} %get-tuple-element.27), channel_id=1, source_target_pairs={{1,2},{3,4},{5,6},{7,8},{9,10},{11,12},{13,14},{15,64},{65,66},{67... | collective-permute-start | bytes 1572872 | tf_op jit(solution)/shard_map/ppermute | solution.py:245
  21.4 13.2 %copy-start.6 = (s32[2,3]{1,0:T(2,128)S(1)}, s32[2,3]{1,0:T(2,128)}, u32[]{:S(2)}) copy-start(s32[2,3]{1,0:T(2,128)} %param.11) | copy-start | bytes 76
  21.4 13.2 %copy-start.5 = (bf16[2,3,128,128]{3,2,1,0:T(8,128)(2,1)S(1)}, bf16[2,3,128,128]{3,2,1,0:T(8,128)(2,1)}, u32[]{:S(2)}) copy-start(bf16[2,3,128,128]{3,2,1,0:T(8,128)(2,1)} %param.10) | copy-start | bytes 589828
  22.7 16.0 %collective-permute-start.5 = (bf16[4,4,64,256]{3,2,1,0:T(8,128)(2,1)S(1)}, bf16[4,4,64,256]{3,2,1,0:T(8,128)(2,1)S(1)}, u32[]{:S(2)}, u32[]{:S(2)}) collective-permute-start(bf16[4,4,64,256]{3,2,1,0:T(8,128)(2,1)S(1)} %get-tuple-element.23.late2), channel_id=1, source_target_pairs={{16,32},{32,16},{17,33},{33,17},{18,34},{34,18},{19,35},{35,19},{2... | collective-permute-start | bytes 1572872 | tf_op jit(solution)/shard_map/ppermute | solution.py:269
  23.4 15.3 %collective-permute-start.6 = (bf16[4,4,64,256]{3,2,1,0:T(8,128)(2,1)S(1)}, bf16[4,4,64,256]{3,2,1,0:T(8,128)(2,1)S(1)}, u32[]{:S(2)}, u32[]{:S(2)}) collective-permute-start(bf16[4,4,64,256]{3,2,1,0:T(8,128)(2,1)S(1)} %get-tuple-element.22.after.late1), channel_id=1, source_target_pairs={{0,16},{32,48},{16,0},{48,32},{1,17},{33,49},{17,1},{49,33},{2,18}... | collective-permute-start | bytes 1572872 | tf_op jit(solution)/shard_map/ppermute | solution.py:270
  27.7 14.2 %collective-permute-start.8 = (bf16[17,64,256]{2,1,0:T(8,128)(2,1)S(1)}, bf16[17,64,256]{2,1,0:T(8,128)(2,1)S(1)}, u32[]{:S(2)}, u32[]{:S(2)}) collective-permute-start(bf16[17,64,256]{2,1,0:T(8,128)(2,1)S(1)} %get-tuple-element.26.refs_4_), channel_id=1, source_target_pairs={{1,2},{3,4},{5,6},{7,8},{9,10},{11,12},{13,14},{15,64},{65,66},{67... | collective-permute-start | bytes 1671176 | tf_op jit(solution)/shard_map/ppermute | solution.py:271
  32.7 7.0 %collective-permute-start.7 = (bf16[16,64,256]{2,1,0:T(8,128)(2,1)S(1)}, bf16[16,64,256]{2,1,0:T(8,128)(2,1)S(1)}, u32[]{:S(2)}, u32[]{:S(2)}) collective-permute-start(bf16[16,64,256]{2,1,0:T(8,128)(2,1)S(1)} %get-tuple-element.30), channel_id=1, source_target_pairs={{0,1},{2,3},{4,5},{6,7},{8,9},{10,11},{12,13},{14,15},{64,65},{66,... | collective-permute-start | bytes 1572872 | tf_op jit(solution)/shard_map/ppermute | solution.py:272

commit v4 on v3

--- a/solution.py
+++ b/solution.py
@@ -40,7 +40,6 @@
             for l in range(4):
                 far2[8 * e + 2 * l + slot] = raw[two + e, l]
                 far1[8 * e + 2 * l + slot] = raw[one + e, l]
-    far2[16] = jnp.zeros(far2.shape[1:], BF16)
 
 
 def weight_kernel(s_ref, occupation, offsets, qtable, early, out, early_out):
@@ -262,13 +261,13 @@
     sent2, sent1 = call(
         far_kernel,
         [SMEM, VMEM, VMEM, ANY],
-        [((17, RAW, 256), BF16), ((16, RAW, 256), BF16)],
+        [((16, RAW, 256), BF16)] * 2,
         (scalars, raw2, raw1, own_late1),
         "far",
     )
     rim_late2 = lax.ppermute(own_late2, "blk", x2)
     rim_late1 = lax.ppermute(own_late1, "blk", x1)
-    far2 = lax.ppermute(sent2, e_axes, y2)
+    far2 = lax.ppermute(sent2.reshape(2, 8, RAW, 256), e_axes, y2).reshape(16, RAW, 256)
     far1 = lax.ppermute(sent1, e_axes, y1)
     own_early1, own_early2 = own(0, 0, early2, sent2, tile_raw, "own_early", 1)
     (inner,) = call(

time: 45.4 us -> 45 us (level)
  no operation moved by 1% of the time
where the time goes in v4:
time: 45 us; the launch traced here: 44.7 us
  starting transfers between devices  29.3 us (65%)
  Pallas kernels  11.4 us (25%)
  waiting for transfers between devices  1.85 us (4%)
  local copies, waits for them, and re-layouts  1.62 us (4%)
    pallas_call x8, Pallas kernels, call(): pl.pallas_call(kernel, in_specs=in_specs, out_specs=out_specs, out_shape=...  11.4 us
    ppermute x1, starting transfers between devices, local(): raw1 = lax.ppermute(raw1, 'blk', x1)  6.1 us
    ppermute x1, starting transfers between devices, local(): late2 = lax.ppermute(late2, e_axes, y2)  6.02 us
    ppermute x1, starting transfers between devices, local(): lax.ppermute(sent2.reshape(2, 8, RAW, 256), e_axes, y2)  4.96 us
    ppermute x1, starting transfers between devices, local(): rim_late1 = lax.ppermute(own_late1, 'blk', x1)  3.67 us
    ppermute x1, starting transfers between devices, local(): early2 = lax.ppermute(early2, e_axes, y2)  3.36 us
    ppermute x1, starting transfers between devices, local(): whole1 = lax.ppermute(whole1, e_axes, y1)  1.92 us
    ppermute x1, starting transfers between devices, local(): far1 = lax.ppermute(sent1, e_axes, y1)  1.92 us
  transfers between devices with their start and end apart: 9, of which 1 were waited for; matrix products, arithmetic and copies ran while one was open for 0% of the time, Pallas kernels for 17%

profile of v4, /device:TPU:512, one launch (start us, length us, event | category | flops | bytes accessed | tf_op | source)
XLA Modules:
  0.0 44.7 jit_solution(16443263507094501278)
XLA Ops:
  0.0 0.1 pad_add_fusion.s_ref.refs_0_
  0.1 1.6 %copy-done = bf16[4,4,2,128,256]{4,3,2,1,0:T(8,128)(2,1)S(1)} copy-done((bf16[4,4,2,128,256]{4,3,2,1,0:T(8,128)(2,1)S(1)}, bf16[4,4,2,128,256]{4,3,2,1,0:T(8,128)(2,1)}, u32[]{:S(2)}) %copy-start) | copy-done | bytes 2097176
  1.7 0.7 %load.1 = (bf16[4,4,64,256]{3,2,1,0:T(8,128)(2,1)S(1)}, bf16[4,4,64,256]{3,2,1,0:T(8,128)(2,1)S(1)}, bf16[2,4,2,64,256]{4,3,2,1,0:T(8,128)(2,1)S(1)}, bf16[2,4,2...) custom-call(s32[3]{0:T(128)S(1)} %pad_add_fusion.s_ref.refs_0_, bf16[4,4,2,128,256]{4,3,2,1,0:T(8,128)(2,1)S(1)} %copy-done), custom_call_target="tpu_custom_call" | custom-call | flops 1 | bytes 1 | tf_op jit(solution)/shard_map/load/pallas_call | solution.py:199
  2.5 6.0 %collective-permute-start.1 = (bf16[2,4,2,64,256]{4,3,2,1,0:T(8,128)(2,1)S(1)}, bf16[2,4,2,64,256]{4,3,2,1,0:T(8,128)(2,1)S(1)}, u32[]{:S(2)}, u32[]{:S(2)}) collective-permute-start(bf16[2,4,2,64,256]{4,3,2,1,0:T(8,128)(2,1)S(1)} %get-tuple-element.21), channel_id=1, source_target_pairs={{1,2},{3,4},{5,6},{7,8},{9,10},{11,12},{13,14},{15,64},{65,66},{67... | collective-permute-start | bytes 1572872 | tf_op jit(solution)/shard_map/ppermute | solution.py:233
  8.5 0.7 %collective-permute-start.2 = (bf16[4,4,64,256]{3,2,1,0:T(8,128)(2,1)S(1)}, bf16[4,4,64,256]{3,2,1,0:T(8,128)(2,1)S(1)}, u32[]{:S(2)}, u32[]{:S(2)}) collective-permute-start(bf16[4,4,64,256]{3,2,1,0:T(8,128)(2,1)S(1)} %get-tuple-element.24), channel_id=1, source_target_pairs={{16,32},{32,16},{17,33},{33,17},{18,34},{34,18},{19,35},{35,19},{2... | collective-permute-start | bytes 1572872 | tf_op jit(solution)/shard_map/ppermute | solution.py:231
  9.2 6.1 %collective-permute-start.3 = (bf16[4,4,64,256]{3,2,1,0:T(8,128)(2,1)S(1)}, bf16[4,4,64,256]{3,2,1,0:T(8,128)(2,1)S(1)}, u32[]{:S(2)}, u32[]{:S(2)}) collective-permute-start(bf16[4,4,64,256]{3,2,1,0:T(8,128)(2,1)S(1)} %get-tuple-element.25), channel_id=1, source_target_pairs={{0,16},{32,48},{16,0},{48,32},{1,17},{33,49},{17,1},{49,33},{2,18}... | collective-permute-start | bytes 1572872 | tf_op jit(solution)/shard_map/ppermute | solution.py:232
  15.3 1.9 %collective-permute-start = (bf16[2,4,2,128,256]{4,3,2,1,0:T(8,128)(2,1)S(1)}, bf16[2,4,2,128,256]{4,3,2,1,0:T(8,128)(2,1)S(1)}, u32[]{:S(2)}, u32[]{:S(2)}) collective-permute-start(bf16[2,4,2,128,256]{4,3,2,1,0:T(8,128)(2,1)S(1)} %get-tuple-element.20), channel_id=1, source_target_pairs={{0,1},{2,3},{4,5},{6,7},{8,9},{10,11},{12,13},{14,15},{64,65},{66,... | collective-permute-start | bytes 3145736 | tf_op jit(solution)/shard_map/ppermute | solution.py:234
  17.2 0.0 copy-start.1
  17.3 0.7 %weights.1 = (bf16[256,512]{1,0:T(8,128)(2,1)S(1)}, bf16[2,4,2,64,256]{4,3,2,1,0:T(8,128)(2,1)S(1)}) custom-call(s32[3]{0:T(128)S(1)} %pad_add_fusion.s_ref.refs_0_, f32[4]{0:T(128)S(1)} %copy-done.3, s32[4]{0:T(128)S(1)} %copy-done.4, s32[4,4]{1,0:T(4,128)S(1)} %copy-done.2, bf16[2,4,2,64,256]{4,3,2,1,0:T(8,128)(2,1)S(1)} %get-tuple-element.18.early), custom_call_target="tpu_custom_call" | custom-call | flops 99999997952 | bytes 1 | tf_op jit(solution)/shard_map/weights/pallas_call | solution.py:199
  18.0 3.4 %collective-permute-start.4 = (bf16[2,4,2,64,256]{4,3,2,1,0:T(8,128)(2,1)S(1)}, bf16[2,4,2,64,256]{4,3,2,1,0:T(8,128)(2,1)S(1)}, u32[]{:S(2)}, u32[]{:S(2)}) collective-permute-start(bf16[2,4,2,64,256]{4,3,2,1,0:T(8,128)(2,1)S(1)} %get-tuple-element.27), channel_id=1, source_target_pairs={{1,2},{3,4},{5,6},{7,8},{9,10},{11,12},{13,14},{15,64},{65,66},{67... | collective-permute-start | bytes 1572872 | tf_op jit(solution)/shard_map/ppermute | solution.py:244
  21.3 0.0 collective-permute-done.1.refs_5_
  21.4 0.0 collective-permute-done.refs_3_.refs_4_
  21.4 0.0 copy-start.6
  21.4 0.0 copy-start.5
  21.4 1.3 %own_late.1 = (bf16[4,4,64,256]{3,2,1,0:T(8,128)(2,1)S(1)}, bf16[4,4,64,256]{3,2,1,0:T(8,128)(2,1)S(1)}) custom-call(s32[3]{0:T(128)S(1)} %pad_add_fusion.s_ref.refs_0_, bf16[256,512]{1,0:T(8,128)(2,1)S(1)} %get-tuple-element.19.refs_1_.weights, bf16[4,4,2,128,256]{4,3,2,1,0:T(8,128)(2,1)S(1)} %copy-done.1, ...), custom_call_target="tpu_custom_call" | custom-call | flops 1 | bytes 1 | tf_op jit(solution)/shard_map/own_late/pallas_call | solution.py:199
  22.7 0.7 %collective-permute-start.5 = (bf16[4,4,64,256]{3,2,1,0:T(8,128)(2,1)S(1)}, bf16[4,4,64,256]{3,2,1,0:T(8,128)(2,1)S(1)}, u32[]{:S(2)}, u32[]{:S(2)}) collective-permute-start(bf16[4,4,64,256]{3,2,1,0:T(8,128)(2,1)S(1)} %get-tuple-element.23.late2), channel_id=1, source_target_pairs={{16,32},{32,16},{17,33},{33,17},{18,34},{34,18},{19,35},{35,19},{2... | collective-permute-start | bytes 1572872 | tf_op jit(solution)/shard_map/ppermute | solution.py:268
  23.4 3.7 %collective-permute-start.6 = (bf16[4,4,64,256]{3,2,1,0:T(8,128)(2,1)S(1)}, bf16[4,4,64,256]{3,2,1,0:T(8,128)(2,1)S(1)}, u32[]{:S(2)}, u32[]{:S(2)}) collective-permute-start(bf16[4,4,64,256]{3,2,1,0:T(8,128)(2,1)S(1)} %get-tuple-element.22.after.late1), channel_id=1, source_target_pairs={{0,16},{32,48},{16,0},{48,32},{1,17},{33,49},{17,1},{49,33},{2,18}... | collective-permute-start | bytes 1572872 | tf_op jit(solution)/shard_map/ppermute | solution.py:269
  27.0 0.0 collective-permute-done.2.raw2
  27.1 0.0 collective-permute-done.3.raw1
  27.1 0.6 %far.1 = (bf16[16,64,256]{2,1,0:T(8,128)(2,1)S(1)}, bf16[16,64,256]{2,1,0:T(8,128)(2,1)S(1)}) custom-call(s32[3]{0:T(128)S(1)} %pad_add_fusion.s_ref.refs_0_, bf16[4,4,64,256]{3,2,1,0:T(8,128)(2,1)S(1)} %collective-permute-done.2.raw2, bf16[4,4,64,256]{3,2,1,0:T(8,128)(2,1)S(1)} %collective-permute-done.3.raw1, ...), custom_call_target="tpu_custom_call" | custom-call | flops 1 | bytes 1 | tf_op jit(solution)/shard_map/far/pallas_call | solution.py:199
  27.7 5.0 %collective-permute-start.8 = (bf16[2,8,64,256]{3,2,1,0:T(8,128)(2,1)S(1)}, bf16[2,8,64,256]{3,2,1,0:T(8,128)(2,1)S(1)}, u32[]{:S(2)}, u32[]{:S(2)}) collective-permute-start(bf16[2,8,64,256]{3,2,1,0:T(8,128)(2,1)S(1)} %bitcast.6), channel_id=1, source_target_pairs={{1,2},{3,4},{5,6},{7,8},{9,10},{11,12},{13,14},{15,64},{65,66},{67... | collective-permute-start | bytes 1572872 | tf_op jit(solution)/shard_map/ppermute | solution.py:270
  32.7 1.9 %collective-permute-start.7 = (bf16[16,64,256]{2,1,0:T(8,128)(2,1)S(1)}, bf16[16,64,256]{2,1,0:T(8,128)(2,1)S(1)}, u32[]{:S(2)}, u32[]{:S(2)}) collective-permute-start(bf16[16,64,256]{2,1,0:T(8,128)(2,1)S(1)} %get-tuple-element.30), channel_id=1, source_target_pairs={{0,1},{2,3},{4,5},{6,7},{8,9},{10,11},{12,13},{14,15},{64,65},{66,... | collective-permute-start | bytes 1572872 | tf_op jit(solution)/shard_map/ppermute | solution.py:271
  34.6 0.1 broadcast_multiply_fusion.eff
  34.7 0.0 collective-permute-done.4.refs_5_
  34.7 1.3 %own_early.1 = (bf16[4,4,64,256]{3,2,1,0:T(8,128)(2,1)S(1)}, bf16[4,4,64,256]{3,2,1,0:T(8,128)(2,1)S(1)}) custom-call(s32[3]{0:T(128)S(1)} %pad_add_fusion.s_ref.refs_0_, bf16[256,512]{1,0:T(8,128)(2,1)S(1)} %get-tuple-element.19.refs_1_.weights, bf16[4,4,2,128,256]{4,3,2,1,0:T(8,128)(2,1)S(1)} %copy-done.1, ...), custom_call_target="tpu_custom_call" | custom-call | flops 1 | bytes 1 | tf_op jit(solution)/shard_map/own_early/pallas_call | solution.py:199
  36.0 2.7 %inner.1 = f32[4,4,2,128,256]{4,3,2,1,0:T(8,128)S(1)} custom-call(s32[3]{0:T(128)S(1)} %pad_add_fusion.s_ref.refs_0_, bf16[2,3,128,128]{3,2,1,0:T(8,128)(2,1)S(1)} %broadcast_multiply_fusion.eff, bf16[4,4,64,256]{3,2,1,0:T(8,128)(2,1)S(1)} %get-tuple-element.22.after.late1, bf16[4,4,64,256]{3,2,1,0:T(8,128)(2,1)S(1)} %get-tuple-element.23.late2, ...), custom_call_target="tpu_custom_call" | custom-call | flops 1 | bytes 1 | tf_op jit(solution)/shard_map/inner/pallas_call | solution.py:199
  38.7 0.0 collective-permute-done.5.late2
  38.7 0.0 collective-permute-done.6.late1
  38.7 1.0 %late.1 = bf16[2,16,64,256]{3,2,1,0:T(8,128)(2,1)S(1)} custom-call(s32[3]{0:T(128)S(1)} %pad_add_fusion.s_ref.refs_0_, bf16[2,3,128,128]{3,2,1,0:T(8,128)(2,1)S(1)} %broadcast_multiply_fusion.eff, bf16[4,4,64,256]{3,2,1,0:T(8,128)(2,1)S(1)} %collective-permute-done.5.late2, bf16[4,4,64,256]{3,2,1,0:T(8,128)(2,1)S(1)} %collective-permute-done.6.late1), custom_call_target="tpu_custom_call" | custom-call | flops 1000000000 | bytes 1 | tf_op jit(solution)/shard_map/late/pallas_call | solution.py:199
  39.7 1.8 %collective-permute-done.8 = bf16[2,8,64,256]{3,2,1,0:T(8,128)(2,1)S(1)} collective-permute-done((bf16[2,8,64,256]{3,2,1,0:T(8,128)(2,1)S(1)}, bf16[2,8,64,256]{3,2,1,0:T(8,128)(2,1)S(1)}, u32[]{:S(2)}, u32[]{:S(2)}) %collective-permute-start.8) | collective-permute-done | bytes 524320 | tf_op jit(solution)/shard_map/ppermute | solution.py:270
  41.5 0.0 collective-permute-done.7.far1
  41.5 3.2 %final.1 = bf16[4,4,2,128,256]{4,3,2,1,0:T(8,128)(2,1)} custom-call(s32[3]{0:T(128)S(1)} %pad_add_fusion.s_ref.refs_0_, bf16[2,3,128,128]{3,2,1,0:T(8,128)(2,1)S(1)} %broadcast_multiply_fusion.eff, f32[4,4,2,128,256]{4,3,2,1,0:T(8,128)S(1)} %inner.1, bf16[2,16,64,256]{3,2,1,0:T(8,128)(2,1)S(1)} %late.1, ...), custom_call_target="tpu_custom_call" | custom-call | flops 1 | bytes 1 | tf_op jit(solution)/shard_map/final/pallas_call | solution.py:199
  (11 shorter events, 0.0 us)
Async XLA Ops:
  0.0 17.2 %copy-start.2 = (s32[4,4]{1,0:T(4,128)S(1)}, s32[4,4]{1,0:T(4,128)}, u32[]{:S(2)}) copy-start(s32[4,4]{1,0:T(4,128)} %qtable.1) | copy-start | bytes 196
  0.0 17.2 %copy-start.4 = (s32[4]{0:T(128)S(1)}, s32[4]{0:T(128)}, u32[]{:S(2)}) copy-start(s32[4]{0:T(128)} %offsets.1) | copy-start | bytes 52
  0.0 17.2 %copy-start.3 = (f32[4]{0:T(128)S(1)}, f32[4]{0:T(128)}, u32[]{:S(2)}) copy-start(f32[4]{0:T(128)} %occupation.1) | copy-start | bytes 52
  0.1 1.6 %copy-start = (bf16[4,4,2,128,256]{4,3,2,1,0:T(8,128)(2,1)S(1)}, bf16[4,4,2,128,256]{4,3,2,1,0:T(8,128)(2,1)}, u32[]{:S(2)}) copy-start(bf16[4,4,2,128,256]{4,3,2,1,0:T(8,128)(2,1)} %refs_2_.3) | copy-start | bytes 6291460
  2.5 18.9 %collective-permute-start.1 = (bf16[2,4,2,64,256]{4,3,2,1,0:T(8,128)(2,1)S(1)}, bf16[2,4,2,64,256]{4,3,2,1,0:T(8,128)(2,1)S(1)}, u32[]{:S(2)}, u32[]{:S(2)}) collective-permute-start(bf16[2,4,2,64,256]{4,3,2,1,0:T(8,128)(2,1)S(1)} %get-tuple-element.21), channel_id=1, source_target_pairs={{1,2},{3,4},{5,6},{7,8},{9,10},{11,12},{13,14},{15,64},{65,66},{67... | collective-permute-start | bytes 1572872 | tf_op jit(solution)/shard_map/ppermute | solution.py:233
  8.5 18.6 %collective-permute-start.2 = (bf16[4,4,64,256]{3,2,1,0:T(8,128)(2,1)S(1)}, bf16[4,4,64,256]{3,2,1,0:T(8,128)(2,1)S(1)}, u32[]{:S(2)}, u32[]{:S(2)}) collective-permute-start(bf16[4,4,64,256]{3,2,1,0:T(8,128)(2,1)S(1)} %get-tuple-element.24), channel_id=1, source_target_pairs={{16,32},{32,16},{17,33},{33,17},{18,34},{34,18},{19,35},{35,19},{2... | collective-permute-start | bytes 1572872 | tf_op jit(solution)/shard_map/ppermute | solution.py:231
  9.2 17.9 %collective-permute-start.3 = (bf16[4,4,64,256]{3,2,1,0:T(8,128)(2,1)S(1)}, bf16[4,4,64,256]{3,2,1,0:T(8,128)(2,1)S(1)}, u32[]{:S(2)}, u32[]{:S(2)}) collective-permute-start(bf16[4,4,64,256]{3,2,1,0:T(8,128)(2,1)S(1)} %get-tuple-element.25), channel_id=1, source_target_pairs={{0,16},{32,48},{16,0},{48,32},{1,17},{33,49},{17,1},{49,33},{2,18}... | collective-permute-start | bytes 1572872 | tf_op jit(solution)/shard_map/ppermute | solution.py:232
  15.3 6.1 %collective-permute-start = (bf16[2,4,2,128,256]{4,3,2,1,0:T(8,128)(2,1)S(1)}, bf16[2,4,2,128,256]{4,3,2,1,0:T(8,128)(2,1)S(1)}, u32[]{:S(2)}, u32[]{:S(2)}) collective-permute-start(bf16[2,4,2,128,256]{4,3,2,1,0:T(8,128)(2,1)S(1)} %get-tuple-element.20), channel_id=1, source_target_pairs={{0,1},{2,3},{4,5},{6,7},{8,9},{10,11},{12,13},{14,15},{64,65},{66,... | collective-permute-start | bytes 3145736 | tf_op jit(solution)/shard_map/ppermute | solution.py:234
  17.2 4.1 %copy-start.1 = (bf16[4,4,2,128,256]{4,3,2,1,0:T(8,128)(2,1)S(1)}, bf16[4,4,2,128,256]{4,3,2,1,0:T(8,128)(2,1)}, u32[]{:S(2)}) copy-start(bf16[4,4,2,128,256]{4,3,2,1,0:T(8,128)(2,1)} %refs_2_.3) | copy-start | bytes 6291460
  18.0 16.7 %collective-permute-start.4 = (bf16[2,4,2,64,256]{4,3,2,1,0:T(8,128)(2,1)S(1)}, bf16[2,4,2,64,256]{4,3,2,1,0:T(8,128)(2,1)S(1)}, u32[]{:S(2)}, u32[]{:S(2)}) collective-permute-start(bf16[2,4,2,64,256]{4,3,2,1,0:T(8,128)(2,1)S(1)} %get-tuple-element.27), channel_id=1, source_target_pairs={{1,2},{3,4},{5,6},{7,8},{9,10},{11,12},{13,14},{15,64},{65,66},{67... | collective-permute-start | bytes 1572872 | tf_op jit(solution)/shard_map/ppermute | solution.py:244
  21.4 13.2 %copy-start.6 = (s32[2,3]{1,0:T(2,128)S(1)}, s32[2,3]{1,0:T(2,128)}, u32[]{:S(2)}) copy-start(s32[2,3]{1,0:T(2,128)} %param.11) | copy-start | bytes 76
  21.4 13.2 %copy-start.5 = (bf16[2,3,128,128]{3,2,1,0:T(8,128)(2,1)S(1)}, bf16[2,3,128,128]{3,2,1,0:T(8,128)(2,1)}, u32[]{:S(2)}) copy-start(bf16[2,3,128,128]{3,2,1,0:T(8,128)(2,1)} %param.10) | copy-start | bytes 589828
  22.7 16.0 %collective-permute-start.5 = (bf16[4,4,64,256]{3,2,1,0:T(8,128)(2,1)S(1)}, bf16[4,4,64,256]{3,2,1,0:T(8,128)(2,1)S(1)}, u32[]{:S(2)}, u32[]{:S(2)}) collective-permute-start(bf16[4,4,64,256]{3,2,1,0:T(8,128)(2,1)S(1)} %get-tuple-element.23.late2), channel_id=1, source_target_pairs={{16,32},{32,16},{17,33},{33,17},{18,34},{34,18},{19,35},{35,19},{2... | collective-permute-start | bytes 1572872 | tf_op jit(solution)/shard_map/ppermute | solution.py:268
  23.4 15.3 %collective-permute-start.6 = (bf16[4,4,64,256]{3,2,1,0:T(8,128)(2,1)S(1)}, bf16[4,4,64,256]{3,2,1,0:T(8,128)(2,1)S(1)}, u32[]{:S(2)}, u32[]{:S(2)}) collective-permute-start(bf16[4,4,64,256]{3,2,1,0:T(8,128)(2,1)S(1)} %get-tuple-element.22.after.late1), channel_id=1, source_target_pairs={{0,16},{32,48},{16,0},{48,32},{1,17},{33,49},{17,1},{49,33},{2,18}... | collective-permute-start | bytes 1572872 | tf_op jit(solution)/shard_map/ppermute | solution.py:269
  27.7 13.8 %collective-permute-start.8 = (bf16[2,8,64,256]{3,2,1,0:T(8,128)(2,1)S(1)}, bf16[2,8,64,256]{3,2,1,0:T(8,128)(2,1)S(1)}, u32[]{:S(2)}, u32[]{:S(2)}) collective-permute-start(bf16[2,8,64,256]{3,2,1,0:T(8,128)(2,1)S(1)} %bitcast.6), channel_id=1, source_target_pairs={{1,2},{3,4},{5,6},{7,8},{9,10},{11,12},{13,14},{15,64},{65,66},{67... | collective-permute-start | bytes 1572872 | tf_op jit(solution)/shard_map/ppermute | solution.py:270
  32.7 8.9 %collective-permute-start.7 = (bf16[16,64,256]{2,1,0:T(8,128)(2,1)S(1)}, bf16[16,64,256]{2,1,0:T(8,128)(2,1)S(1)}, u32[]{:S(2)}, u32[]{:S(2)}) collective-permute-start(bf16[16,64,256]{2,1,0:T(8,128)(2,1)S(1)} %get-tuple-element.30), channel_id=1, source_target_pairs={{0,1},{2,3},{4,5},{6,7},{8,9},{10,11},{12,13},{14,15},{64,65},{66,... | collective-permute-start | bytes 1572872 | tf_op jit(solution)/shard_map/ppermute | solution.py:271
